TPU v7x, 256 devices: a whole 4x4x8 slice. The times are simulated.
256 devices in a mesh: dp: 32 (over y, x, core), seq: 8 (over z).
Axes of the slice: x: 4, y: 4, z: 8, core: 2. Of those that a mesh axis runs over, the one named last changes fastest.
Arguments:
- features: bfloat16 [64, 24, 32, 1536], P('dp', 'seq'), may hold values from -6 to 6
- enc_gain: float32 [1536], replicated, may hold values from 0.25 to 4
- enc_bias: float32 [1536], replicated, may hold values from -0.02 to 0.02
- row_source: int32 [64, 48], P('dp', 'seq'), may hold values from 0 to 22, as said below
- timesteps: int32 [64], P('dp'), may hold values from 0 to 999
- pre_act: bfloat16 [64, 48, 64, 2048], P('dp', 'seq'), may hold values from -8 to 8
- proj_weight: bfloat16 [2048, 1536], P('dp'), may hold values from -0.125 to 0.125
- proj_bias: float32 [1536], replicated, may hold values from -3 to 3
Outputs:
- pre_grad: bfloat16 [64, 48, 64, 2048], P('dp', 'seq')
- weight_grad: float32 [2048, 1536], P('dp')
Inputs may be any that keep to these rules, and one draw needn't show every extreme that they name: row_source[b, r] lies between r // 2 - 2 and r // 2 + 1.
All inputs are finite; a program needn't handle non-finite values.
Results may differ from a plain program's by a relative error of at most 0.0057.
Values may be sent and summed in bfloat16 or wider, within the bound.
No kernel may reach another device: no remote copies, remote signals or barrier semaphores. Data moves between devices by JAX's collectives and lax.ppermute only.
A program may use at most 128 MiB of HBM per device.

v0:
```python
import functools

import jax
import jax.numpy as jnp
from jax import lax
from jax.experimental import pallas as pl
from jax.experimental.pallas import tpu as pltpu
from jax.sharding import Mesh, PartitionSpec as P

loss_scale = 1024.0
norm_eps = 1e-06
MIB = 1 << 20
bf16, f32 = jnp.bfloat16, jnp.float32
VMEM = pltpu.VMEM
SMEM = pltpu.SMEM


def shift(block, axis, step):
    count = lax.axis_size(axis)
    return lax.ppermute(block, axis, [(i, (i + step) % count) for i in range(count)])


def turn(block, order, step):
    pairs = []
    for y in range(4):
        for x in range(4):
            for c in range(2):
                along_x = (c == 0) == (order == 0)
                to_y, to_x = (y, (x + step) % 4) if along_x else ((y + step) % 4, x)
                pairs.append(((y * 4 + x) * 2 + c, (to_y * 4 + to_x) * 2 + c))
    return lax.ppermute(block, ("y", "x", "c"), pairs)


FIRST, SECOND = 0, 1
LINE = (0, 3, 1, 2)
ORDER = (2, 1, 3, 0)


def params(mib, steps=0):
    semantics = ("arbitrary",) * steps if steps else None
    return pltpu.CompilerParams(vmem_limit_bytes=mib * MIB, dimension_semantics=semantics)


def cost(flops, nbytes, trans=0):
    return pl.CostEstimate(flops=flops // 64, bytes_accessed=nbytes // 64, transcendentals=trans // 64)


def gate_kernel(*refs):
    pass


def gate(arrays, after):
    anywhere = pl.BlockSpec(memory_space=pl.ANY)
    return pl.pallas_call(
        gate_kernel,
        in_specs=[anywhere] * (len(arrays) + len(after)),
        out_specs=[anywhere] * len(arrays),
        out_shape=[jax.ShapeDtypeStruct(array.shape, array.dtype) for array in arrays],
        input_output_aliases={k: k for k in range(len(arrays))},
        compiler_params=params(1),
        cost_estimate=cost(0, 0),
        name="gate",
    )(*arrays, *after)


def pack_kernel(own_ref, left_ref, right_ref, far_ref, after_ref, out_ref):
    for k, ref in enumerate((own_ref, left_ref, right_ref, far_ref)):
        out_ref[k * 64 : k * 64 + 64, :] = ref[...]


def pack(own, left, right, far, after):
    whole = pl.BlockSpec(memory_space=VMEM)
    return pl.pallas_call(
        pack_kernel,
        in_specs=[whole] * 4 + [pl.BlockSpec(memory_space=pl.ANY)],
        out_specs=whole,
        out_shape=jax.ShapeDtypeStruct((256, own.shape[1]), bf16),
        compiler_params=params(4),
        cost_estimate=cost(0, MIB),
        name="pack",
    )(own, left, right, far, after)


def spot_of(core, second, first, my_y, my_x):
    y = jnp.where(core == 0, my_y + second, my_y + first) % 4
    x = jnp.where(core == 0, my_x + first, my_x + second) % 4
    return y * 4 + x


def here():
    return lax.axis_index("y"), lax.axis_index("x"), lax.axis_index("c")


def silu_kernel(pre_ref, rows_ref, act_ref):
    step = pl.program_id(0)
    my_y, my_x, my_c = here()
    dy = (step // 4 - my_y + 4) % 4
    dx = (step % 4 - my_x + 4) % 4
    p = pre_ref[...].astype(f32)
    active = (p * jax.nn.sigmoid(p)).astype(bf16)
    turned = active.T
    for c in range(2):
        dc = (c - my_c + 2) % 2
        second, first = (dy, dx) if c == 0 else (dx, dy)
        block = jnp.where(second == 2, 0, jnp.where(second == 0, 3, jnp.where(second == 1, 1, 2)))
        spot = jnp.where(first == 0, 0, jnp.where(first == 3, 1, first + 1))
        row = pl.multiple_of(dc * 1024 + block * 256 + spot * 64, 64)
        rows_ref[pl.ds(row, 64), :] = turned[c * 64 : c * 64 + 64, :]

    @pl.when(step == pl.num_programs(0) - 1)
    def _():
        for at, k in enumerate((0, 1, 8, 9, 2, 3, 4, 5, 6, 7, 10, 11, 12, 13, 14, 15)):
            act_ref[:, at * 128 : at * 128 + 128] = rows_ref[k * 128 : k * 128 + 128, :].T


def hidden_rows(pre):
    tokens, hidden = pre.shape
    return pl.pallas_call(
        silu_kernel,
        grid=(hidden // 128,),
        in_specs=[pl.BlockSpec((tokens, 128), lambda i: (0, i))],
        out_specs=[
            pl.BlockSpec((hidden, tokens), lambda i: (0, 0)),
            pl.BlockSpec((tokens, hidden), lambda i: (0, 0)),
        ],
        out_shape=[jax.ShapeDtypeStruct((hidden, tokens), bf16), jax.ShapeDtypeStruct((tokens, hidden), bf16)],
        compiler_params=params(20, 1),
        cost_estimate=cost(tokens * hidden * 8, tokens * hidden * 6, tokens * hidden),
        name="hidden_rows",
    )(pre)


def target_kernel(source_ref, left_ref, mid_ref, right_ref, gain_ref, bias_ref, after_ref, out_ref, sum_ref, ext_ref):
    gain, bias = gain_ref[...].reshape(1, -1), bias_ref[...].reshape(1, -1)
    width = gain.shape[-1]
    offset = lax.axis_index("z") * 3 - 2
    for b in range(2):
        row = 0
        for ref, count in ((left_ref, 2), (mid_ref, 3), (right_ref, 2)):
            for k in range(count):
                x = ref[b, k].astype(f32)
                center = x - jnp.sum(x, axis=-1, keepdims=True) * (1.0 / width)
                spread = jnp.sum(center * center, axis=-1, keepdims=True) * (1.0 / width)
                ext_ref[b, row : row + 32, :] = (center * lax.rsqrt(spread + norm_eps) * gain + bias).astype(bf16)
                row += 32
    c = lax.broadcasted_iota(jnp.int32, (64, 224), 0)
    lane = lax.broadcasted_iota(jnp.int32, (64, 224), 1)
    source, j = lane // 32, lane % 32
    odd = c % 2 == 1
    low = jnp.where(odd, (c - 1) // 2, c // 2 - 1)
    high_w = jnp.where(odd, 0.25, 0.75).astype(f32)
    columns = jnp.where(j == jnp.clip(low, 0, 31), 1.0 - high_w, 0.0) + jnp.where(
        j == jnp.clip(low + 1, 0, 31), high_w, 0.0
    )
    for b in range(2):
        for r in range(6):
            h = 0.25 if r % 2 == 1 else 0.75
            first = source_ref[b, r] - offset
            rows = jnp.where(source == first, 1.0 - h, 0.0) + jnp.where(source == first + 1, h, 0.0)
            blend = (columns * rows).astype(bf16)
            target = jnp.dot(blend, ext_ref[b], preferred_element_type=f32)
            at = (b * 6 + r) * 64
            out_ref[at : at + 64, :] = target
            sum_ref[at : at + 64, :] = jnp.broadcast_to(jnp.sum(target * target, axis=-1, keepdims=True), (64, 128))


def make_target(row_source, left, mid, right, gain, bias, after):
    width = gain.shape[-1]
    whole = pl.BlockSpec(memory_space=VMEM)
    return pl.pallas_call(
        target_kernel,
        in_specs=[pl.BlockSpec(memory_space=SMEM)] + [whole] * 5 + [pl.BlockSpec(memory_space=pl.ANY)],
        out_specs=[whole, whole],
        out_shape=[jax.ShapeDtypeStruct((768, width), f32), jax.ShapeDtypeStruct((768, 128), f32)],
        scratch_shapes=[pltpu.VMEM((2, 224, width), bf16)],
        compiler_params=params(16),
        cost_estimate=cost(2 * 768 * 224 * width, 768 * width * 8),
        name="make_target",
    )(row_source, left, mid, right, gain, bias, after)


def near_kernel(first, has_base, act_ref, base_ref, *refs):
    pieces, (out_ref, w_ref, sem_ref) = refs[:3], refs[-3:]
    copies = [
        pltpu.make_async_copy(piece_ref, w_ref.at[k * 256 : k * 256 + 256], sem_ref.at[k])
        for k, piece_ref in enumerate(pieces)
    ]
    for copy in copies:
        copy.start()
    for copy in copies:
        copy.wait()
    step = 256
    for n in range(out_ref.shape[1] // step):
        at = slice(n * step, n * step + step)
        base = base_ref[:, at] if has_base else base_ref[at].reshape(1, -1)
        out_ref[:, at] = base + jnp.dot(act_ref[:, first : first + 768], w_ref[:, at], preferred_element_type=f32)


def near_part(active, base, pieces, first, after):
    tokens = active.shape[0]
    width = base.shape[-1]
    whole = pl.BlockSpec(memory_space=VMEM)
    anywhere = pl.BlockSpec(memory_space=pl.ANY)
    return pl.pallas_call(
        functools.partial(near_kernel, first, base.ndim == 2),
        in_specs=[whole] * 2 + [anywhere] * 4,
        out_specs=whole,
        out_shape=jax.ShapeDtypeStruct((tokens, width), f32),
        scratch_shapes=[pltpu.VMEM((768, width), bf16), pltpu.SemaphoreType.DMA((3,))],
        compiler_params=params(12),
        cost_estimate=cost(2 * tokens * 768 * width, 8 * MIB),
        name="near_part",
    )(active, base, *pieces, after)


def grad_kernel(time_ref, near_ref, act_ref, target_ref, tsum_ref, *refs):
    pieces, (out_ref, proj_ref, pp_ref, pt_ref, w_ref, sem_ref) = refs[:4], refs[4:]
    copies = [
        pltpu.make_async_copy(piece_ref, w_ref.at[k * 128 : k * 128 + 128], sem_ref.at[k])
        for k, piece_ref in enumerate(pieces)
    ]
    for copy in copies:
        copy.start()
    for copy in copies:
        copy.wait()
    width = out_ref.shape[1]
    step = 256
    pp_ref[...] = jnp.zeros_like(pp_ref)
    pt_ref[...] = jnp.zeros_like(pt_ref)

    for n in range(width // step):
        at = slice(n * step, n * step + step)
        proj = near_ref[:, at] + jnp.dot(act_ref[:, 0:512], w_ref[:, at], preferred_element_type=f32)
        proj_ref[:, at] = proj
        target = target_ref[:, at]
        square, cross = proj * proj, proj * target
        pp_ref[...] += square[:, :128] + square[:, 128:]
        pt_ref[...] += cross[:, :128] + cross[:, 128:]

    half_tokens = out_ref.shape[0] // 2
    for part in range(12):
        rows = slice(part * 64, part * 64 + 64)
        scaled = -loss_scale * (1.0 - time_ref[part * 64 // half_tokens].astype(f32) * 0.001)
        pn2 = jnp.sum(pp_ref[rows, :], axis=-1, keepdims=True) + norm_eps
        pt = jnp.sum(pt_ref[rows, :], axis=-1, keepdims=True)
        tn2 = tsum_ref[rows, 0:1] + norm_eps
        inv = lax.rsqrt(pn2) * lax.rsqrt(tn2)
        near = scaled * inv
        along = scaled * (pt * inv) / pn2
        out_ref[rows, :] = (near * target_ref[rows, :] - along * proj_ref[rows, :]).astype(bf16)


def out_grads(timesteps, near, active, target, tsum, pieces):
    tokens, width = target.shape
    whole = pl.BlockSpec(memory_space=VMEM)
    smem = pl.BlockSpec(memory_space=SMEM)
    return pl.pallas_call(
        grad_kernel,
        in_specs=[smem] + [whole] * 4 + [pl.BlockSpec(memory_space=pl.ANY)] * len(pieces),
        out_specs=whole,
        out_shape=jax.ShapeDtypeStruct((tokens, width), bf16),
        scratch_shapes=[
            pltpu.VMEM((tokens, width), f32),
            pltpu.VMEM((tokens, 128), f32),
            pltpu.VMEM((tokens, 128), f32),
            pltpu.VMEM((512, width), bf16),
            pltpu.SemaphoreType.DMA((4,)),
        ],
        compiler_params=params(20),
        cost_estimate=cost(2 * tokens * 512 * width, 15 * MIB),
        name="out_grads",
    )(timesteps, near, active, target, tsum, *pieces)


def outer_kernel(first, blocks, outs, added, *refs):
    rows_ref, grad_ref = refs[:2]
    extra_ref = refs[2] if added else None
    out_refs = refs[-len(outs) :]
    step = 256

    for n in range(grad_ref.shape[1] // step):
        at = slice(n * step, n * step + step)
        value = jnp.dot(rows_ref[first : first + blocks * 256, :], grad_ref[:, at], preferred_element_type=f32)
        if extra_ref is not None:
            value = value + extra_ref[:, at].astype(f32)
        for (start, count, dtype), out_ref in zip(outs, out_refs):
            out_ref[:, at] = value[start : start + count].astype(dtype)


def outer(rows, grad, start, count, outs, extra=None, after=None):
    tokens, width = grad.shape
    whole = pl.BlockSpec(memory_space=VMEM)
    inputs = [rows, grad] + ([] if extra is None else [extra])
    specs = [whole] * len(inputs)
    if after is not None:
        inputs, specs = inputs + [after], specs + [pl.BlockSpec(memory_space=pl.ANY)]
    return pl.pallas_call(
        functools.partial(outer_kernel, start, count // 256, outs, extra is not None),
        in_specs=specs,
        out_specs=[whole] * len(outs),
        out_shape=[jax.ShapeDtypeStruct((n, width), dtype) for _, n, dtype in outs],
        compiler_params=params(12),
        cost_estimate=cost(2 * count * tokens * width, 4 * MIB),
        name="outer",
    )(*inputs)


def whole_kernel(*refs):
    pieces, (w_ref, held_ref, sem_ref) = refs[:10], refs[-3:]
    my_y, my_x, my_c = here()
    copies, at, spots = [], 0, []
    for k, piece_ref in enumerate(pieces):
        count = piece_ref.shape[0]
        copies.append(pltpu.make_async_copy(piece_ref, held_ref.at[at : at + count], sem_ref.at[k]))
        at += count
    for copy in copies:
        copy.start()
    at = 0
    for copy, piece_ref in zip(copies, pieces):
        copy.wait()
        for _ in range(piece_ref.shape[0] // 64):
            core = (my_c + at // 1024) % 2
            row = spot_of(core, ORDER[at // 256 % 4], LINE[at // 64 % 4], my_y, my_x) * 128 + core * 64
            w_ref[pl.ds(pl.multiple_of(row, 64), 64), :] = held_ref[at : at + 64, :]
            at += 64


def whole_weight(pieces, after):
    width = pieces[0].shape[1]
    anywhere = pl.BlockSpec(memory_space=pl.ANY)
    return pl.pallas_call(
        whole_kernel,
        in_specs=[anywhere] * 11,
        out_specs=pl.BlockSpec(memory_space=VMEM),
        out_shape=jax.ShapeDtypeStruct((2048, width), bf16),
        scratch_shapes=[pltpu.VMEM((2048, width), bf16), pltpu.SemaphoreType.DMA((10,))],
        compiler_params=params(10),
        cost_estimate=cost(0, 12 * MIB),
        name="whole_weight",
    )(*pieces, after)


def pre_kernel(grad_ref, w_ref, pre_ref, *refs):
    out_ref = refs[-1]
    step = 256
    for k in range(pre_ref.shape[1] // step):
        at = slice(k * step, k * step + step)
        back = lax.dot_general(
            grad_ref[...], w_ref[at, :], (((1,), (1,)), ((), ())), preferred_element_type=f32
        )
        p = pre_ref[:, at].astype(f32)
        s = jax.nn.sigmoid(p)
        out_ref[:, at] = (back * (s * (1.0 + p * (1.0 - s)))).astype(bf16)


def pre_grads(grad, weight, pre, start, count, after, old=None):
    tokens, width = grad.shape
    hidden = weight.shape[0]
    step = 512
    first = start // step
    anywhere = pl.BlockSpec(memory_space=pl.ANY)
    inputs = [grad, weight, pre, after] + ([] if old is None else [old])
    block = pl.BlockSpec((tokens, step), lambda i: (0, first + i))
    return pl.pallas_call(
        pre_kernel,
        grid=(count // step,),
        in_specs=[
            pl.BlockSpec((tokens, width), lambda i: (0, 0)),
            pl.BlockSpec((step, width), lambda i: (first + i, 0)),
            block,
        ]
        + [anywhere] * (len(inputs) - 3),
        out_specs=block,
        out_shape=jax.ShapeDtypeStruct((tokens, hidden), bf16),
        input_output_aliases={} if old is None else {4: 0},
        compiler_params=params(20, 1),
        cost_estimate=cost(2 * tokens * count * width, 8 * MIB),
        name="pre_grads",
    )(*inputs)


def summed(own, blocks, axis):
    right, left, far = blocks
    return (
        own
        + turn(right, axis, 1).astype(f32)
        + turn(left, axis, -1).astype(f32)
        + turn(far, axis, 2).astype(f32)
    )


def body(features, enc_gain, enc_bias, row_source, timesteps, pre_act, proj_weight, proj_bias):
    width = proj_weight.shape[1]
    pre = pre_act.reshape(-1, pre_act.shape[-1])
    line = [proj_weight, turn(proj_weight, FIRST, 1), turn(proj_weight, FIRST, -1), turn(proj_weight, FIRST, 2)]
    left = shift(features[:, 1:], "z", 1)
    right = shift(features[:, :2], "z", -1)
    rows, active = hidden_rows(pre)
    line = pack(*line, rows)
    three, one = turn(line, SECOND, 1), turn(line, SECOND, -1)
    three, one = gate((three, one), (left, right))
    target, tsum = make_target(row_source, left, features, right, enc_gain, enc_bias, line)
    two = [turn(three[:128], SECOND, 1), turn(one[128:], SECOND, -1)]
    mine = [one, three, line]
    other = [shift(piece, "c", 1) for piece in mine]
    close = near_part(active, proj_bias, mine, 512, one)
    close = near_part(active, close, other, 1280, one)
    two = list(gate(two, (close, tsum)))
    other_two = [shift(piece, "c", 1) for piece in two]
    grad = out_grads(timesteps, close, active, target, tsum, two + other_two)
    (away_far,) = outer(rows, grad, 1024, 256, ((0, 256, bf16),))
    back_far = shift(away_far, "c", 1)
    (away,) = outer(rows, grad, 1280, 768, ((0, 768, bf16),), after=away_far)
    (away,) = gate((away,), (back_far,))
    back = shift(away, "c", 1)
    (far,) = outer(rows, grad, 0, 256, ((0, 256, bf16),), back_far, after=away)
    kept_outs = ((0, 256, bf16), (256, 256, bf16), (512, 256, f32))
    to_one, to_three, own = outer(rows, grad, 256, 768, kept_outs, back, after=far)
    weight = whole_weight(two + mine + other_two + other, to_one)
    pre_grad = pre_grads(grad, weight, pre, 0, 1536, to_three)
    (own,) = gate((own,), (pre_grad,))
    own = summed(own, (to_one, to_three, far), SECOND)
    blocks = {first: own[k * 64 : k * 64 + 64] for k, first in enumerate(LINE)}
    block = summed(blocks[0], [blocks[d].astype(bf16) for d in (1, 3, 2)], FIRST).astype(bf16)
    parts = lax.all_to_all(block, "z", 0, 0, tiled=True)
    pre_grad = pre_grads(grad, weight, pre, 1536, 512, block, pre_grad)
    (parts,) = gate((parts,), (pre_grad,))
    total = jnp.sum(parts.reshape(8, 8, width).astype(f32), axis=0).astype(bf16)
    total = jnp.broadcast_to(total[None], (8, 8, width)).reshape(block.shape)
    weight_grad = lax.all_to_all(total, "z", 0, 0, tiled=True).astype(f32)
    return (pre_grad.reshape(pre_act.shape), weight_grad)


def solution(mesh):
    fine = Mesh(mesh.devices.reshape(4, 4, 2, 8), ("y", "x", "c", "z"))
    dp = ("y", "x", "c")
    return jax.shard_map(
        body,
        mesh=fine,
        in_specs=(
            P(dp, "z", None, None),
            P(),
            P(),
            P(dp, "z"),
            P(dp),
            P(dp, "z", None, None),
            P(dp, None),
            P(),
        ),
        out_specs=(P(dp, "z", None, None), P(dp, None)),
        check_vma=False,
    )
```

profile of v0, /device:TPU:6, one launch (start us, length us, event | category | flops | bytes accessed | tf_op | source)
XLA Modules:
  0.0 117.1 jit_solution(10479908439322267881)
XLA Ops:
  0.6 2.3 %collective-permute-start = (bf16[64,1536]{1,0:T(8,128)(2,1)}, bf16[64,1536]{1,0:T(8,128)(2,1)S(1)}, u32[]{:S(2)}, u32[]{:S(2)}) collective-permute-start(bf16[64,1536]{1,0:T(8,128)(2,1)} %own_ref.1), channel_id=1, source_target_pairs={{0,16},{8,72},{16,32},{24,88},{32,48},{40,104},{48,0},{56,120},{64... | collective-permute-start | bytes 589832 | tf_op jit(solution)/shard_map/ppermute | solution.py:31
  2.9 1.5 %collective-permute-start.2 = (bf16[64,1536]{1,0:T(8,128)(2,1)}, bf16[64,1536]{1,0:T(8,128)(2,1)S(1)}, u32[]{:S(2)}, u32[]{:S(2)}) collective-permute-start(bf16[64,1536]{1,0:T(8,128)(2,1)} %own_ref.1), channel_id=1, source_target_pairs={{0,32},{8,136},{16,48},{24,152},{32,0},{40,168},{48,16},{56,184},{... | collective-permute-start | bytes 589832 | tf_op jit(solution)/shard_map/ppermute | solution.py:31
  4.5 1.9 %copy-done.4 = bf16[2,6,64,2048]{3,2,1,0:T(8,128)(2,1)S(1)} copy-done((bf16[2,6,64,2048]{3,2,1,0:T(8,128)(2,1)S(1)}, bf16[2,6,64,2048]{3,2,1,0:T(8,128)(2,1)}, u32[]{:S(2)}) %copy-start.4) | copy-done | bytes 3145752
  6.4 4.0 %hidden_rows.1 = (bf16[2048,768]{1,0:T(8,128)(2,1)S(1)}, bf16[768,2048]{1,0:T(8,128)(2,1)S(1)}) custom-call(bf16[768,2048]{1,0:T(8,128)(2,1)S(1)} %bitcast.10), custom_call_target="tpu_custom_call" | custom-call | flops 196608 | bytes 147456 | tf_op jit(solution)/shard_map/hidden_rows/pallas_call | solution.py:118
  10.3 1.8 %collective-permute-done.1.right_ref = bf16[64,1536]{1,0:T(8,128)(2,1)S(1)} collective-permute-done((bf16[64,1536]{1,0:T(8,128)(2,1)}, bf16[64,1536]{1,0:T(8,128)(2,1)S(1)}, u32[]{:S(2)}, u32[]{:S(2)}) %collective-permute-start.1) | collective-permute-done | bytes 196640 | tf_op jit(solution)/shard_map/ppermute | solution.py:31
  12.3 3.2 %collective-permute-start.4 = (bf16[256,1536]{1,0:T(8,128)(2,1)S(1)}, bf16[256,1536]{1,0:T(8,128)(2,1)S(1)}, u32[]{:S(2)}, u32[]{:S(2)}) collective-permute-start(bf16[256,1536]{1,0:T(8,128)(2,1)S(1)} %pack.1.refs_2_.after_ref.refs_4_), channel_id=1, source_target_pairs={{0,192},{8,56},{16,208},{24,8},{32,224},{40,24},{48,240},{56,40},{... | collective-permute-start | bytes 2359304 | tf_op jit(solution)/shard_map/ppermute | solution.py:31
  15.9 4.0 %collective-permute-start.6 = (bf16[2,2,32,1536]{3,2,1,0:T(8,128)(2,1)S(1)}, bf16[2,2,32,1536]{3,2,1,0:T(8,128)(2,1)S(1)}, u32[]{:S(2)}, u32[]{:S(2)}) collective-permute-start(bf16[2,2,32,1536]{3,2,1,0:T(8,128)(2,1)S(1)} %get-tuple-element.29), channel_id=1, source_target_pairs={{0,7},{1,0},{2,1},{3,2},{4,3},{5,4},{6,5},{7,6},{8,15},{9,8},{10,9... | collective-permute-start | bytes 1179656 | tf_op jit(solution)/shard_map/ppermute | solution.py:20
  19.9 7.9 %collective-permute-done.5.refs_2_.left_ref = bf16[2,2,32,1536]{3,2,1,0:T(8,128)(2,1)S(1)} collective-permute-done((bf16[2,2,32,1536]{3,2,1,0:T(8,128)(2,1)S(1)}, bf16[2,2,32,1536]{3,2,1,0:T(8,128)(2,1)S(1)}, u32[]{:S(2)}, u32[]{:S(2)}) %collective-permute-start.5) | collective-permute-done | bytes 393248 | tf_op jit(solution)/shard_map/ppermute | solution.py:20
  30.6 2.9 %make_target.1 = (f32[768,1536]{1,0:T(8,128)S(1)}, f32[768,128]{1,0:T(8,128)S(1)}) custom-call(s32[2,6]{1,0:T(2,128)S(1)} %copy-done.12, bf16[2,2,32,1536]{3,2,1,0:T(8,128)(2,1)S(1)} %collective-permute-done.5.refs_2_.left_ref, bf16[2,3,32,1536]{3,2,1,0:T(8,128)(2,1)S(1)} %copy-done.7, bf16[2,2,32,1536]{3,2,1,0:T(8,128)(2,1)S(1)} %collective-permute-done.6.refs_3_.right_ref, ...), custom_call_target="tpu_custom_call" | custom-call | flops 8257536 | bytes 147456 | tf_op jit(solution)/shard_map/make_target/pallas_call | solution.py:170
  33.5 2.2 %near_part.2.base_ref = f32[768,1536]{1,0:T(8,128)S(1)} custom-call(bf16[768,2048]{1,0:T(8,128)(2,1)S(1)} %get-tuple-element.13.act_ref, f32[1536]{0:T(1024)S(1)} %copy-done.11, bf16[256,1536]{1,0:T(8,128)(2,1)S(1)} %get-tuple-element.15.refs_0_.refs_3_.refs_2_, bf16[256,1536]{1,0:T(8,128)(2,1)S(1)} %get-tuple-element.16.refs_1_.refs_3_, ...), custom_call_target="tpu_custom_call" | custom-call | flops 28311552 | bytes 131072 | tf_op jit(solution)/shard_map/near_part/pallas_call | solution.py:204
  35.7 2.2 %near_part.3.refs_2_.near_ref = f32[768,1536]{1,0:T(8,128)S(1)} custom-call(bf16[768,2048]{1,0:T(8,128)(2,1)S(1)} %get-tuple-element.13.act_ref, f32[768,1536]{1,0:T(8,128)S(1)} %near_part.2.base_ref, bf16[256,1536]{1,0:T(8,128)(2,1)S(1)} %collective-permute-done.7.refs_0_.refs_7_, bf16[256,1536]{1,0:T(8,128)(2,1)S(1)} %collective-permute-done.8.refs_1_.refs_8_, ...), custom_call_target="tpu_custom_call" | custom-call | flops 28311552 | bytes 131072 | tf_op jit(solution)/shard_map/near_part/pallas_call | solution.py:204
  41.0 4.4 %out_grads.1.refs_1_.grad_ref = bf16[768,1536]{1,0:T(8,128)(2,1)S(1)} custom-call(s32[2]{0:T(128)S(1)} %copy-done.13, f32[768,1536]{1,0:T(8,128)S(1)} %near_part.3.refs_2_.near_ref, bf16[768,2048]{1,0:T(8,128)(2,1)S(1)} %get-tuple-element.13.act_ref, f32[768,1536]{1,0:T(8,128)S(1)} %get-tuple-element.17.target_ref, ...), custom_call_target="tpu_custom_call" | custom-call | flops 18874368 | bytes 245760 | tf_op jit(solution)/shard_map/out_grads/pallas_call | solution.py:257
  46.4 2.0 %outer.5.refs_0_ = bf16[768,1536]{1,0:T(8,128)(2,1)S(1)} custom-call(bf16[2048,768]{1,0:T(8,128)(2,1)S(1)} %get-tuple-element.14.after_ref.refs_0_, bf16[768,1536]{1,0:T(8,128)(2,1)S(1)} %out_grads.1.refs_1_.grad_ref, bf16[256,1536]{1,0:T(8,128)(2,1)S(1)} %outer.4.refs_2_), custom_call_target="tpu_custom_call" | custom-call | flops 28311552 | bytes 65536 | tf_op jit(solution)/shard_map/outer/pallas_call | solution.py:297
  49.7 1.8 %collective-permute-start.18 = (bf16[256,1536]{1,0:T(8,128)(2,1)S(1)}, bf16[256,1536]{1,0:T(8,128)(2,1)S(1)}, u32[]{:S(2)}, u32[]{:S(2)}) collective-permute-start(bf16[256,1536]{1,0:T(8,128)(2,1)S(1)} %outer.6.refs_3_), channel_id=1, source_target_pairs={{0,128},{8,40},{16,144},{24,56},{32,160},{40,8},{48,176},{56,24},{... | collective-permute-start | bytes 2359304 | tf_op jit(solution)/shard_map/ppermute | solution.py:31
  51.5 1.6 %collective-permute-done.15.refs_2_ = bf16[768,1536]{1,0:T(8,128)(2,1)S(1)} collective-permute-done((bf16[768,1536]{1,0:T(8,128)(2,1)S(1)}, bf16[768,1536]{1,0:T(8,128)(2,1)S(1)}, u32[]{:S(2)}, u32[]{:S(2)}) %collective-permute-start.15) | collective-permute-done | bytes 2359328 | tf_op jit(solution)/shard_map/ppermute | solution.py:20
  53.1 2.0 %outer.7 = (bf16[256,1536]{1,0:T(8,128)(2,1)S(1)}, bf16[256,1536]{1,0:T(8,128)(2,1)S(1)}, f32[256,1536]{1,0:T(8,128)S(1)}) custom-call(bf16[2048,768]{1,0:T(8,128)(2,1)S(1)} %get-tuple-element.14.after_ref.refs_0_, bf16[768,1536]{1,0:T(8,128)(2,1)S(1)} %out_grads.1.refs_1_.grad_ref, bf16[768,1536]{1,0:T(8,128)(2,1)S(1)} %collective-permute-done.15.refs_2_, ...), custom_call_target="tpu_custom_call" | custom-call | flops 28311552 | bytes 65536 | tf_op jit(solution)/shard_map/outer/pallas_call | solution.py:297
  55.8 2.6 %collective-permute-start.17 = (bf16[256,1536]{1,0:T(8,128)(2,1)S(1)}, bf16[256,1536]{1,0:T(8,128)(2,1)S(1)}, u32[]{:S(2)}, u32[]{:S(2)}) collective-permute-start(bf16[256,1536]{1,0:T(8,128)(2,1)S(1)} %get-tuple-element.23.refs_0_), channel_id=1, source_target_pairs={{0,192},{8,56},{16,208},{24,8},{32,224},{40,24},{48,240},{56,40},{... | collective-permute-start | bytes 2359304 | tf_op jit(solution)/shard_map/ppermute | solution.py:31
  58.4 1.7 %whole_weight.1.w_ref = bf16[2048,1536]{1,0:T(8,128)(2,1)S(1)} custom-call(bf16[128,1536]{1,0:T(8,128)(2,1)S(1)} %get-tuple-element.19.refs_0_, bf16[128,1536]{1,0:T(8,128)(2,1)S(1)} %get-tuple-element.20.refs_1_, bf16[256,1536]{1,0:T(8,128)(2,1)S(1)} %get-tuple-element.15.refs_0_.refs_3_.refs_2_, bf16[256,1536]{1,0:T(8,128)(2,1)S(1)} %get-tuple-element.16.refs_1_.refs_3_, ...), custom_call_target="tpu_custom_call" | custom-call | bytes 196608 | tf_op jit(solution)/shard_map/whole_weight/pallas_call | solution.py:331
  60.1 6.0 %pre_grads.2.refs_1_ = bf16[768,2048]{1,0:T(8,128)(2,1)} custom-call(bf16[768,1536]{1,0:T(8,128)(2,1)S(1)} %out_grads.1.refs_1_.grad_ref, bf16[2048,1536]{1,0:T(8,128)(2,1)S(1)} %whole_weight.1.w_ref, bf16[768,2048]{1,0:T(8,128)(2,1)S(1)} %bitcast.11, bf16[256,1536]{1,0:T(8,128)(2,1)S(1)} %get-tuple-element.23.refs_0_), custom_call_target="tpu_custom_call" | custom-call | flops 56623104 | bytes 131072 | tf_op jit(solution)/shard_map/pre_grads/pallas_call | solution.py:364
  66.2 1.9 %copy-done.2 = bf16[768,2048]{1,0:T(8,128)(2,1)S(1)} copy-done((bf16[768,2048]{1,0:T(8,128)(2,1)S(1)}, bf16[768,2048]{1,0:T(8,128)(2,1)}, u32[]{:S(2)}) %copy-start.2) | copy-done | bytes 3145752
  68.1 3.8 %collective-permute-done.16 = bf16[256,1536]{1,0:T(8,128)(2,1)S(1)} collective-permute-done((bf16[256,1536]{1,0:T(8,128)(2,1)S(1)}, bf16[256,1536]{1,0:T(8,128)(2,1)S(1)}, u32[]{:S(2)}, u32[]{:S(2)}) %collective-permute-start.16) | collective-permute-done | bytes 786464 | tf_op jit(solution)/shard_map/ppermute | solution.py:31
  72.4 1.7 %collective-permute-start.19 = (bf16[64,1536]{1,0:T(8,128)(2,1)S(1)}, bf16[64,1536]{1,0:T(8,128)(2,1)S(1)}, u32[]{:S(2)}, u32[]{:S(2)}) collective-permute-start(bf16[64,1536]{1,0:T(8,128)(2,1)S(1)} %get-tuple-element.26), channel_id=1, source_target_pairs={{0,16},{8,72},{16,32},{24,88},{32,48},{40,104},{48,0},{56,120},{64... | collective-permute-start | bytes 589832 | tf_op jit(solution)/shard_map/ppermute | solution.py:31
  74.5 1.3 %collective-permute-start.21 = (bf16[64,1536]{1,0:T(8,128)(2,1)S(1)}, bf16[64,1536]{1,0:T(8,128)(2,1)S(1)}, u32[]{:S(2)}, u32[]{:S(2)}) collective-permute-start(bf16[64,1536]{1,0:T(8,128)(2,1)S(1)} %get-tuple-element.27), channel_id=1, source_target_pairs={{0,32},{8,136},{16,48},{24,152},{32,0},{40,168},{48,16},{56,184},{... | collective-permute-start | bytes 589832 | tf_op jit(solution)/shard_map/ppermute | solution.py:31
  75.8 2.3 %collective-permute-done.19 = bf16[64,1536]{1,0:T(8,128)(2,1)S(1)} collective-permute-done((bf16[64,1536]{1,0:T(8,128)(2,1)S(1)}, bf16[64,1536]{1,0:T(8,128)(2,1)S(1)}, u32[]{:S(2)}, u32[]{:S(2)}) %collective-permute-start.19) | collective-permute-done | bytes 196640 | tf_op jit(solution)/shard_map/ppermute | solution.py:31
  78.2 4.9 %collective-permute-done.20 = bf16[64,1536]{1,0:T(8,128)(2,1)S(1)} collective-permute-done((bf16[64,1536]{1,0:T(8,128)(2,1)S(1)}, bf16[64,1536]{1,0:T(8,128)(2,1)S(1)}, u32[]{:S(2)}, u32[]{:S(2)}) %collective-permute-start.20) | collective-permute-done | bytes 196640 | tf_op jit(solution)/shard_map/ppermute | solution.py:31
  83.9 6.6 %all-to-all-start = ((bf16[8,8,1536]{2,1,0:T(8,128)(2,1)}), bf16[8,8,1536]{2,1,0:T(8,128)(2,1)S(1)}, u32[]{:S(2)}, u32[]{:S(2)}) async-start(bf16[8,8,1536]{2,1,0:T(8,128)(2,1)} %bitcast.2), calls=%async_computation | async-start | bytes 393216 | tf_op jit(solution)/shard_map/all_to_all | solution.py:425
  90.4 2.8 %copy-done.1 = bf16[2048,1536]{1,0:T(8,128)(2,1)S(1)} copy-done((bf16[2048,1536]{1,0:T(8,128)(2,1)S(1)}, bf16[2048,1536]{1,0:T(8,128)(2,1)}, u32[]{:S(2)}) %copy-start.1) | copy-done | bytes 6291480
  93.2 1.9 %copy-done.6 = bf16[2,6,64,2048]{3,2,1,0:T(8,128)(2,1)S(1)} copy-done((bf16[2,6,64,2048]{3,2,1,0:T(8,128)(2,1)S(1)}, bf16[2,6,64,2048]{3,2,1,0:T(8,128)(2,1)}, u32[]{:S(2)}) %copy-start.6) | copy-done | bytes 3145752
  95.1 2.5 %pre_grads.3.refs_1_ = bf16[768,2048]{1,0:T(8,128)(2,1)} custom-call(bf16[768,1536]{1,0:T(8,128)(2,1)S(1)} %out_grads.1.refs_1_.grad_ref, bf16[2048,1536]{1,0:T(8,128)(2,1)S(1)} %copy-done.1, bf16[768,2048]{1,0:T(8,128)(2,1)S(1)} %bitcast.12, bf16[64,1536]{1,0:T(8,128)(2,1)} %fusion.2.refs_0_, ...), custom_call_target="tpu_custom_call", output_to_operand_aliasing={{}: (4, {})} | custom-call | flops 18874368 | bytes 131072 | tf_op jit(solution)/shard_map/pre_grads/pallas_call | solution.py:364
  97.6 2.6 %all-to-all-done = bf16[8,8,1536]{2,1,0:T(8,128)(2,1)S(1)} async-done(((bf16[8,8,1536]{2,1,0:T(8,128)(2,1)}), bf16[8,8,1536]{2,1,0:T(8,128)(2,1)S(1)}, u32[]{:S(2)}, u32[]{:S(2)}) %all-to-all-start) | async-done | bytes 196640 | tf_op jit(solution)/shard_map/all_to_all | solution.py:425
  100.2 1.9 %copy-done.3 = bf16[768,2048]{1,0:T(8,128)(2,1)S(1)} copy-done((bf16[768,2048]{1,0:T(8,128)(2,1)S(1)}, bf16[768,2048]{1,0:T(8,128)(2,1)}, u32[]{:S(2)}) %copy-start.3) | copy-done | bytes 3145752
  102.2 14.2 %all_to_all.17 = bf16[8,8,1536]{2,1,0:T(8,128)(2,1)S(1)} all-to-all(bf16[8,8,1536]{2,1,0:T(8,128)(2,1)S(1)} %broadcast_in_dim.2), channel_id=1, replica_groups=mesh['y'=4,'x'=4,'c'=2,'z'=8] {'z'}, dimensions={0} | all-to-all | bytes 393216 | tf_op jit(solution)/shard_map/all_to_all | solution.py:430
  (70 shorter events, 11.8 us)
Async XLA Ops:
  0.6 9.7 %collective-permute-start = (bf16[64,1536]{1,0:T(8,128)(2,1)}, bf16[64,1536]{1,0:T(8,128)(2,1)S(1)}, u32[]{:S(2)}, u32[]{:S(2)}) collective-permute-start(bf16[64,1536]{1,0:T(8,128)(2,1)} %own_ref.1), channel_id=1, source_target_pairs={{0,16},{8,72},{16,32},{24,88},{32,48},{40,104},{48,0},{56,120},{64... | collective-permute-start | bytes 589832 | tf_op jit(solution)/shard_map/ppermute | solution.py:31
  2.9 9.2 %collective-permute-start.1 = (bf16[64,1536]{1,0:T(8,128)(2,1)}, bf16[64,1536]{1,0:T(8,128)(2,1)S(1)}, u32[]{:S(2)}, u32[]{:S(2)}) collective-permute-start(bf16[64,1536]{1,0:T(8,128)(2,1)} %own_ref.1), channel_id=1, source_target_pairs={{0,48},{8,200},{16,0},{24,216},{32,16},{40,232},{48,32},{56,248},{... | collective-permute-start | bytes 589832 | tf_op jit(solution)/shard_map/ppermute | solution.py:31
  2.9 9.2 %collective-permute-start.2 = (bf16[64,1536]{1,0:T(8,128)(2,1)}, bf16[64,1536]{1,0:T(8,128)(2,1)S(1)}, u32[]{:S(2)}, u32[]{:S(2)}) collective-permute-start(bf16[64,1536]{1,0:T(8,128)(2,1)} %own_ref.1), channel_id=1, source_target_pairs={{0,32},{8,136},{16,48},{24,152},{32,0},{40,168},{48,16},{56,184},{... | collective-permute-start | bytes 589832 | tf_op jit(solution)/shard_map/ppermute | solution.py:31
  6.4 5.8 %copy-start.8 = (bf16[64,1536]{1,0:T(8,128)(2,1)S(1)}, bf16[64,1536]{1,0:T(8,128)(2,1)}, u32[]{:S(2)}) copy-start(bf16[64,1536]{1,0:T(8,128)(2,1)} %own_ref.1) | copy-start | bytes 589828
  12.1 3.4 %copy-start.7 = (bf16[2,3,32,1536]{3,2,1,0:T(8,128)(2,1)S(1)}, bf16[2,3,32,1536]{3,2,1,0:T(8,128)(2,1)}, u32[]{:S(2)}) copy-start(bf16[2,3,32,1536]{3,2,1,0:T(8,128)(2,1)} %mid_ref.1) | copy-start | bytes 1769476
  12.2 15.6 %collective-permute-start.3 = (bf16[256,1536]{1,0:T(8,128)(2,1)S(1)}, bf16[256,1536]{1,0:T(8,128)(2,1)S(1)}, u32[]{:S(2)}, u32[]{:S(2)}) collective-permute-start(bf16[256,1536]{1,0:T(8,128)(2,1)S(1)} %pack.1.refs_2_.after_ref.refs_4_), channel_id=1, source_target_pairs={{0,64},{8,24},{16,80},{24,40},{32,96},{40,56},{48,112},{56,8},{64,... | collective-permute-start | bytes 2359304 | tf_op jit(solution)/shard_map/ppermute | solution.py:31
  12.3 15.5 %collective-permute-start.4 = (bf16[256,1536]{1,0:T(8,128)(2,1)S(1)}, bf16[256,1536]{1,0:T(8,128)(2,1)S(1)}, u32[]{:S(2)}, u32[]{:S(2)}) collective-permute-start(bf16[256,1536]{1,0:T(8,128)(2,1)S(1)} %pack.1.refs_2_.after_ref.refs_4_), channel_id=1, source_target_pairs={{0,192},{8,56},{16,208},{24,8},{32,224},{40,24},{48,240},{56,40},{... | collective-permute-start | bytes 2359304 | tf_op jit(solution)/shard_map/ppermute | solution.py:31
  15.6 15.0 %copy-start.9 = (f32[1536]{0:T(1024)S(1)}, f32[1536]{0:T(1024)}, u32[]{:S(2)}) copy-start(f32[1536]{0:T(1024)} %gain_ref.1) | copy-start | bytes 18436
  15.6 15.0 %copy-start.10 = (f32[1536]{0:T(1024)S(1)}, f32[1536]{0:T(1024)}, u32[]{:S(2)}) copy-start(f32[1536]{0:T(1024)} %bias_ref.1) | copy-start | bytes 18436
  15.6 15.0 %copy-start.12 = (s32[2,6]{1,0:T(2,128)S(1)}, s32[2,6]{1,0:T(2,128)}, u32[]{:S(2)}) copy-start(s32[2,6]{1,0:T(2,128)} %source_ref.1) | copy-start | bytes 148
  15.6 12.1 %collective-permute-start.5 = (bf16[2,2,32,1536]{3,2,1,0:T(8,128)(2,1)S(1)}, bf16[2,2,32,1536]{3,2,1,0:T(8,128)(2,1)S(1)}, u32[]{:S(2)}, u32[]{:S(2)}) collective-permute-start(bf16[2,2,32,1536]{3,2,1,0:T(8,128)(2,1)S(1)} %get-tuple-element.30), channel_id=1, source_target_pairs={{0,1},{1,2},{2,3},{3,4},{4,5},{5,6},{6,7},{7,0},{8,9},{9,10},{10,1... | collective-permute-start | bytes 1179656 | tf_op jit(solution)/shard_map/ppermute | solution.py:20
  15.9 11.9 %collective-permute-start.6 = (bf16[2,2,32,1536]{3,2,1,0:T(8,128)(2,1)S(1)}, bf16[2,2,32,1536]{3,2,1,0:T(8,128)(2,1)S(1)}, u32[]{:S(2)}, u32[]{:S(2)}) collective-permute-start(bf16[2,2,32,1536]{3,2,1,0:T(8,128)(2,1)S(1)} %get-tuple-element.29), channel_id=1, source_target_pairs={{0,7},{1,0},{2,1},{3,2},{4,3},{5,4},{6,5},{7,6},{8,15},{9,8},{10,9... | collective-permute-start | bytes 1179656 | tf_op jit(solution)/shard_map/ppermute | solution.py:20
  19.9 15.8 %collective-permute-start.9 = (bf16[256,1536]{1,0:T(8,128)(2,1)S(1)}, bf16[256,1536]{1,0:T(8,128)(2,1)S(1)}, u32[]{:S(2)}, u32[]{:S(2)}) collective-permute-start(bf16[256,1536]{1,0:T(8,128)(2,1)S(1)} %pack.1.refs_2_.after_ref.refs_4_), channel_id=1, source_target_pairs={{0,8},{8,0},{1,9},{9,1},{2,10},{10,2},{3,11},{11,3},{4,12},{12,4},... | collective-permute-start | bytes 2359304 | tf_op jit(solution)/shard_map/ppermute | solution.py:20
  27.8 5.7 %copy-start.11 = (f32[1536]{0:T(1024)S(1)}, f32[1536]{0:T(1024)}, u32[]{:S(2)}) copy-start(f32[1536]{0:T(1024)} %base_ref.1) | copy-start | bytes 18436
  27.8 7.9 %collective-permute-start.7 = (bf16[256,1536]{1,0:T(8,128)(2,1)S(1)}, bf16[256,1536]{1,0:T(8,128)(2,1)S(1)}, u32[]{:S(2)}, u32[]{:S(2)}) collective-permute-start(bf16[256,1536]{1,0:T(8,128)(2,1)S(1)} %get-tuple-element.15.refs_0_.refs_3_.refs_2_), channel_id=1, source_target_pairs={{0,8},{8,0},{1,9},{9,1},{2,10},{10,2},{3,11},{11,3},{4,12},{12,4},... | collective-permute-start | bytes 2359304 | tf_op jit(solution)/shard_map/ppermute | solution.py:20
  27.9 7.8 %collective-permute-start.8 = (bf16[256,1536]{1,0:T(8,128)(2,1)S(1)}, bf16[256,1536]{1,0:T(8,128)(2,1)S(1)}, u32[]{:S(2)}, u32[]{:S(2)}) collective-permute-start(bf16[256,1536]{1,0:T(8,128)(2,1)S(1)} %get-tuple-element.16.refs_1_.refs_3_), channel_id=1, source_target_pairs={{0,8},{8,0},{1,9},{9,1},{2,10},{10,2},{3,11},{11,3},{4,12},{12,4},... | collective-permute-start | bytes 2359304 | tf_op jit(solution)/shard_map/ppermute | solution.py:20
  28.4 9.5 %collective-permute-start.11 = (bf16[128,1536]{1,0:T(8,128)(2,1)S(1)}, bf16[128,1536]{1,0:T(8,128)(2,1)S(1)}, u32[]{:S(2)}, u32[]{:S(2)}) collective-permute-start(bf16[128,1536]{1,0:T(8,128)(2,1)S(1)} %slice.30), channel_id=1, source_target_pairs={{0,192},{8,56},{16,208},{24,8},{32,224},{40,24},{48,240},{56,40},{... | collective-permute-start | bytes 1179656 | tf_op jit(solution)/shard_map/ppermute | solution.py:31
  29.7 9.0 %collective-permute-start.10 = (bf16[128,1536]{1,0:T(8,128)(2,1)S(1)}, bf16[128,1536]{1,0:T(8,128)(2,1)S(1)}, u32[]{:S(2)}, u32[]{:S(2)}) collective-permute-start(bf16[128,1536]{1,0:T(8,128)(2,1)S(1)} %slice.29), channel_id=1, source_target_pairs={{0,64},{8,24},{16,80},{24,40},{32,96},{40,56},{48,112},{56,8},{64,... | collective-permute-start | bytes 1179656 | tf_op jit(solution)/shard_map/ppermute | solution.py:31
  38.7 1.7 %collective-permute-start.12 = (bf16[128,1536]{1,0:T(8,128)(2,1)S(1)}, bf16[128,1536]{1,0:T(8,128)(2,1)S(1)}, u32[]{:S(2)}, u32[]{:S(2)}) collective-permute-start(bf16[128,1536]{1,0:T(8,128)(2,1)S(1)} %get-tuple-element.19.refs_0_), channel_id=1, source_target_pairs={{0,8},{8,0},{1,9},{9,1},{2,10},{10,2},{3,11},{11,3},{4,12},{12,4},... | collective-permute-start | bytes 1179656 | tf_op jit(solution)/shard_map/ppermute | solution.py:20
  38.8 2.2 %collective-permute-start.13 = (bf16[128,1536]{1,0:T(8,128)(2,1)S(1)}, bf16[128,1536]{1,0:T(8,128)(2,1)S(1)}, u32[]{:S(2)}, u32[]{:S(2)}) collective-permute-start(bf16[128,1536]{1,0:T(8,128)(2,1)S(1)} %get-tuple-element.20.refs_1_), channel_id=1, source_target_pairs={{0,8},{8,0},{1,9},{9,1},{2,10},{10,2},{3,11},{11,3},{4,12},{12,4},... | collective-permute-start | bytes 1179656 | tf_op jit(solution)/shard_map/ppermute | solution.py:20
  46.2 2.4 %collective-permute-start.14 = (bf16[256,1536]{1,0:T(8,128)(2,1)S(1)}, bf16[256,1536]{1,0:T(8,128)(2,1)S(1)}, u32[]{:S(2)}, u32[]{:S(2)}) collective-permute-start(bf16[256,1536]{1,0:T(8,128)(2,1)S(1)} %outer.4.refs_2_), channel_id=1, source_target_pairs={{0,8},{8,0},{1,9},{9,1},{2,10},{10,2},{3,11},{11,3},{4,12},{12,4},... | collective-permute-start | bytes 2359304 | tf_op jit(solution)/shard_map/ppermute | solution.py:20
  48.6 4.5 %collective-permute-start.15 = (bf16[768,1536]{1,0:T(8,128)(2,1)S(1)}, bf16[768,1536]{1,0:T(8,128)(2,1)S(1)}, u32[]{:S(2)}, u32[]{:S(2)}) collective-permute-start(bf16[768,1536]{1,0:T(8,128)(2,1)S(1)} %gate.7.refs_3_), channel_id=1, source_target_pairs={{0,8},{8,0},{1,9},{9,1},{2,10},{10,2},{3,11},{11,3},{4,12},{12,4},... | collective-permute-start | bytes 7077896 | tf_op jit(solution)/shard_map/ppermute | solution.py:20
  49.7 18.4 %collective-permute-start.18 = (bf16[256,1536]{1,0:T(8,128)(2,1)S(1)}, bf16[256,1536]{1,0:T(8,128)(2,1)S(1)}, u32[]{:S(2)}, u32[]{:S(2)}) collective-permute-start(bf16[256,1536]{1,0:T(8,128)(2,1)S(1)} %outer.6.refs_3_), channel_id=1, source_target_pairs={{0,128},{8,40},{16,144},{24,56},{32,160},{40,8},{48,176},{56,24},{... | collective-permute-start | bytes 2359304 | tf_op jit(solution)/shard_map/ppermute | solution.py:31
  55.1 16.8 %collective-permute-start.16 = (bf16[256,1536]{1,0:T(8,128)(2,1)S(1)}, bf16[256,1536]{1,0:T(8,128)(2,1)S(1)}, u32[]{:S(2)}, u32[]{:S(2)}) collective-permute-start(bf16[256,1536]{1,0:T(8,128)(2,1)S(1)} %get-tuple-element.21.refs_10_), channel_id=1, source_target_pairs={{0,64},{8,24},{16,80},{24,40},{32,96},{40,56},{48,112},{56,8},{64,... | collective-permute-start | bytes 2359304 | tf_op jit(solution)/shard_map/ppermute | solution.py:31
  55.8 4.3 %copy-start.5 = (bf16[2,6,64,2048]{3,2,1,0:T(8,128)(2,1)S(1)}, bf16[2,6,64,2048]{3,2,1,0:T(8,128)(2,1)}, u32[]{:S(2)}) copy-start(bf16[2,6,64,2048]{3,2,1,0:T(8,128)(2,1)} %param.13) | copy-start | bytes 9437188
  55.8 16.1 %collective-permute-start.17 = (bf16[256,1536]{1,0:T(8,128)(2,1)S(1)}, bf16[256,1536]{1,0:T(8,128)(2,1)S(1)}, u32[]{:S(2)}, u32[]{:S(2)}) collective-permute-start(bf16[256,1536]{1,0:T(8,128)(2,1)S(1)} %get-tuple-element.23.refs_0_), channel_id=1, source_target_pairs={{0,192},{8,56},{16,208},{24,8},{32,224},{40,24},{48,240},{56,40},{... | collective-permute-start | bytes 2359304 | tf_op jit(solution)/shard_map/ppermute | solution.py:31
  60.1 6.0 %copy-start = (bf16[2048,1536]{1,0:T(8,128)(2,1)}, bf16[2048,1536]{1,0:T(8,128)(2,1)S(1)}, u32[]{:S(2)}) copy-start(bf16[2048,1536]{1,0:T(8,128)(2,1)S(1)} %whole_weight.1.w_ref) | copy-start | bytes 18874372
  72.4 5.7 %collective-permute-start.19 = (bf16[64,1536]{1,0:T(8,128)(2,1)S(1)}, bf16[64,1536]{1,0:T(8,128)(2,1)S(1)}, u32[]{:S(2)}, u32[]{:S(2)}) collective-permute-start(bf16[64,1536]{1,0:T(8,128)(2,1)S(1)} %get-tuple-element.26), channel_id=1, source_target_pairs={{0,16},{8,72},{16,32},{24,88},{32,48},{40,104},{48,0},{56,120},{64... | collective-permute-start | bytes 589832 | tf_op jit(solution)/shard_map/ppermute | solution.py:31
  74.1 9.0 %collective-permute-start.20 = (bf16[64,1536]{1,0:T(8,128)(2,1)S(1)}, bf16[64,1536]{1,0:T(8,128)(2,1)S(1)}, u32[]{:S(2)}, u32[]{:S(2)}) collective-permute-start(bf16[64,1536]{1,0:T(8,128)(2,1)S(1)} %get-tuple-element.28), channel_id=1, source_target_pairs={{0,48},{8,200},{16,0},{24,216},{32,16},{40,232},{48,32},{56,248},{... | collective-permute-start | bytes 589832 | tf_op jit(solution)/shard_map/ppermute | solution.py:31
  74.5 8.5 %collective-permute-start.21 = (bf16[64,1536]{1,0:T(8,128)(2,1)S(1)}, bf16[64,1536]{1,0:T(8,128)(2,1)S(1)}, u32[]{:S(2)}, u32[]{:S(2)}) collective-permute-start(bf16[64,1536]{1,0:T(8,128)(2,1)S(1)} %get-tuple-element.27), channel_id=1, source_target_pairs={{0,32},{8,136},{16,48},{24,152},{32,0},{40,168},{48,16},{56,184},{... | collective-permute-start | bytes 589832 | tf_op jit(solution)/shard_map/ppermute | solution.py:31
  83.9 16.4 %all-to-all-start = ((bf16[8,8,1536]{2,1,0:T(8,128)(2,1)}), bf16[8,8,1536]{2,1,0:T(8,128)(2,1)S(1)}, u32[]{:S(2)}, u32[]{:S(2)}) async-start(bf16[8,8,1536]{2,1,0:T(8,128)(2,1)} %bitcast.2), calls=%async_computation | async-start | bytes 393216 | tf_op jit(solution)/shard_map/all_to_all | solution.py:425
  90.4 2.8 %copy-start.1 = (bf16[2048,1536]{1,0:T(8,128)(2,1)S(1)}, bf16[2048,1536]{1,0:T(8,128)(2,1)}, u32[]{:S(2)}) copy-start(bf16[2048,1536]{1,0:T(8,128)(2,1)} %copy-done) | copy-start | bytes 18874372
  (5 other events, 9.9 us)
where the time goes:
time: 118 us; the launch traced here: 117 us
  Pallas kernels  31.6 us (27%)
  starting transfers between devices  30.3 us (26%)
  waiting for transfers between devices  27.6 us (23%)
  blocking collectives  14.2 us (12%)
  local copies, waits for them, and re-layouts  10.5 us (9%)
  other arithmetic  2.04 us (2%)
    ppermute x13, starting transfers between devices, turn(): return lax.ppermute(block, ('y', 'x', 'c'), pairs)  17.8 us
    all_to_all x1, blocking collectives, body(): weight_grad = lax.all_to_all(total, 'z', 0, 0, tiled=True).astype(f32)  14.2 us
    ppermute x13, waiting for transfers between devices, turn(): return lax.ppermute(block, ('y', 'x', 'c'), pairs)  13.6 us
    ppermute x9, waiting for transfers between devices, shift(): lax.ppermute(block, axis, [(i, (i + step) % count) for i in range(count)])  11.4 us
    unnamed x28, local copies, waits for them, and re-layouts  10.4 us
    pallas_call x2, Pallas kernels, pre_grads(): pl.pallas_call(pre_kernel, grid=(count // step,), in_specs=[pl.BlockSpec(...  8.56 us
    all_to_all x1, starting transfers between devices, body(): parts = lax.all_to_all(block, 'z', 0, 0, tiled=True)  6.58 us
    ppermute x9, starting transfers between devices, shift(): lax.ppermute(block, axis, [(i, (i + step) % count) for i in range(count)])  5.93 us
  transfers between devices with their start and end apart: 23, of which 11 were waited for; matrix products, arithmetic and copies ran while one was open for 0% of the time, Pallas kernels for 22%

commit v1 on v0

--- a/solution.py
+++ b/solution.py
@@ -109,7 +109,7 @@
 
     @pl.when(step == pl.num_programs(0) - 1)
     def _():
-        for at, k in enumerate((0, 1, 8, 9, 2, 3, 4, 5, 6, 7, 10, 11, 12, 13, 14, 15)):
+        for at, k in enumerate((6, 7, 14, 15, 2, 3, 4, 5, 0, 1, 10, 11, 12, 13, 8, 9)):
             act_ref[:, at * 128 : at * 128 + 128] = rows_ref[k * 128 : k * 128 + 128, :].T
 
 
@@ -180,7 +180,7 @@
 
 
 def near_kernel(first, has_base, act_ref, base_ref, *refs):
-    pieces, (out_ref, w_ref, sem_ref) = refs[:3], refs[-3:]
+    pieces, (out_ref, w_ref, sem_ref) = refs[:-4], refs[-3:]
     copies = [
         pltpu.make_async_copy(piece_ref, w_ref.at[k * 256 : k * 256 + 256], sem_ref.at[k])
         for k, piece_ref in enumerate(pieces)
@@ -193,7 +193,7 @@
     for n in range(out_ref.shape[1] // step):
         at = slice(n * step, n * step + step)
         base = base_ref[:, at] if has_base else base_ref[at].reshape(1, -1)
-        out_ref[:, at] = base + jnp.dot(act_ref[:, first : first + 768], w_ref[:, at], preferred_element_type=f32)
+        out_ref[:, at] = base + jnp.dot(act_ref[:, first : first + w_ref.shape[0]], w_ref[:, at], preferred_element_type=f32)
 
 
 def near_part(active, base, pieces, first, after):
@@ -203,10 +203,10 @@
     anywhere = pl.BlockSpec(memory_space=pl.ANY)
     return pl.pallas_call(
         functools.partial(near_kernel, first, base.ndim == 2),
-        in_specs=[whole] * 2 + [anywhere] * 4,
+        in_specs=[whole] * 2 + [anywhere] * (len(pieces) + 1),
         out_specs=whole,
         out_shape=jax.ShapeDtypeStruct((tokens, width), f32),
-        scratch_shapes=[pltpu.VMEM((768, width), bf16), pltpu.SemaphoreType.DMA((3,))],
+        scratch_shapes=[pltpu.VMEM((256 * len(pieces), width), bf16), pltpu.SemaphoreType.DMA((len(pieces),))],
         compiler_params=params(12),
         cost_estimate=cost(2 * tokens * 768 * width, 8 * MIB),
         name="near_part",
@@ -214,9 +214,9 @@
 
 
 def grad_kernel(time_ref, near_ref, act_ref, target_ref, tsum_ref, *refs):
-    pieces, (out_ref, proj_ref, pp_ref, pt_ref, w_ref, sem_ref) = refs[:4], refs[4:]
+    pieces, (out_ref, proj_ref, pp_ref, pt_ref, w_ref, sem_ref) = refs[:1], refs[1:]
     copies = [
-        pltpu.make_async_copy(piece_ref, w_ref.at[k * 128 : k * 128 + 128], sem_ref.at[k])
+        pltpu.make_async_copy(piece_ref, w_ref.at[k * 256 : k * 256 + 256], sem_ref.at[k])
         for k, piece_ref in enumerate(pieces)
     ]
     for copy in copies:
@@ -230,7 +230,7 @@
 
     for n in range(width // step):
         at = slice(n * step, n * step + step)
-        proj = near_ref[:, at] + jnp.dot(act_ref[:, 0:512], w_ref[:, at], preferred_element_type=f32)
+        proj = near_ref[:, at] + jnp.dot(act_ref[:, 1792:2048], w_ref[:, at], preferred_element_type=f32)
         proj_ref[:, at] = proj
         target = target_ref[:, at]
         square, cross = proj * proj, proj * target
@@ -263,8 +263,8 @@
             pltpu.VMEM((tokens, width), f32),
             pltpu.VMEM((tokens, 128), f32),
             pltpu.VMEM((tokens, 128), f32),
-            pltpu.VMEM((512, width), bf16),
-            pltpu.SemaphoreType.DMA((4,)),
+            pltpu.VMEM((256, width), bf16),
+            pltpu.SemaphoreType.DMA((1,)),
         ],
         compiler_params=params(20),
         cost_estimate=cost(2 * tokens * 512 * width, 15 * MIB),
@@ -306,7 +306,7 @@
 
 
 def whole_kernel(*refs):
-    pieces, (w_ref, held_ref, sem_ref) = refs[:10], refs[-3:]
+    pieces, (w_ref, held_ref, sem_ref) = refs[:8], refs[-3:]
     my_y, my_x, my_c = here()
     copies, at, spots = [], 0, []
     for k, piece_ref in enumerate(pieces):
@@ -330,10 +330,10 @@
     anywhere = pl.BlockSpec(memory_space=pl.ANY)
     return pl.pallas_call(
         whole_kernel,
-        in_specs=[anywhere] * 11,
+        in_specs=[anywhere] * 9,
         out_specs=pl.BlockSpec(memory_space=VMEM),
         out_shape=jax.ShapeDtypeStruct((2048, width), bf16),
-        scratch_shapes=[pltpu.VMEM((2048, width), bf16), pltpu.SemaphoreType.DMA((10,))],
+        scratch_shapes=[pltpu.VMEM((2048, width), bf16), pltpu.SemaphoreType.DMA((8,))],
         compiler_params=params(10),
         cost_estimate=cost(0, 12 * MIB),
         name="whole_weight",
@@ -341,7 +341,7 @@
 
 
 def pre_kernel(grad_ref, w_ref, pre_ref, *refs):
-    out_ref = refs[-1]
+    out_ref, token_ref = refs[-2:]
     step = 256
     for k in range(pre_ref.shape[1] // step):
         at = slice(k * step, k * step + step)
@@ -351,30 +351,30 @@
         p = pre_ref[:, at].astype(f32)
         s = jax.nn.sigmoid(p)
         out_ref[:, at] = (back * (s * (1.0 + p * (1.0 - s)))).astype(bf16)
-
-
-def pre_grads(grad, weight, pre, start, count, after, old=None):
+    token_ref[...] = jnp.zeros_like(token_ref)
+
+
+def pre_grads(grad, weight, pre, first, count, after, old=None):
     tokens, width = grad.shape
     hidden = weight.shape[0]
     step = 512
-    first = start // step
+    block = pl.BlockSpec((tokens, step), lambda i: (0, first + i))
     anywhere = pl.BlockSpec(memory_space=pl.ANY)
     inputs = [grad, weight, pre, after] + ([] if old is None else [old])
-    block = pl.BlockSpec((tokens, step), lambda i: (0, first + i))
     return pl.pallas_call(
         pre_kernel,
-        grid=(count // step,),
+        grid=(count,),
         in_specs=[
             pl.BlockSpec((tokens, width), lambda i: (0, 0)),
             pl.BlockSpec((step, width), lambda i: (first + i, 0)),
             block,
         ]
         + [anywhere] * (len(inputs) - 3),
-        out_specs=block,
-        out_shape=jax.ShapeDtypeStruct((tokens, hidden), bf16),
+        out_specs=[block, pl.BlockSpec((8, 128), lambda i: (0, 0))],
+        out_shape=[jax.ShapeDtypeStruct((tokens, hidden), bf16), jax.ShapeDtypeStruct((8, 128), f32)],
         input_output_aliases={} if old is None else {4: 0},
         compiler_params=params(20, 1),
-        cost_estimate=cost(2 * tokens * count * width, 8 * MIB),
+        cost_estimate=cost(2 * tokens * step * count * width, 4 * MIB * count),
         name="pre_grads",
     )(*inputs)
 
@@ -393,21 +393,20 @@
     width = proj_weight.shape[1]
     pre = pre_act.reshape(-1, pre_act.shape[-1])
     line = [proj_weight, turn(proj_weight, FIRST, 1), turn(proj_weight, FIRST, -1), turn(proj_weight, FIRST, 2)]
-    left = shift(features[:, 1:], "z", 1)
-    right = shift(features[:, :2], "z", -1)
     rows, active = hidden_rows(pre)
     line = pack(*line, rows)
-    three, one = turn(line, SECOND, 1), turn(line, SECOND, -1)
-    three, one = gate((three, one), (left, right))
+    three, one, two = turn(line, SECOND, 1), turn(line, SECOND, -1), turn(line, SECOND, 2)
+    other_line = shift(line, "c", 1)
+    left, right = gate((features[:, 1:], features[:, :2]), (other_line,))
+    left, right = shift(left, "z", 1), shift(right, "z", -1)
     target, tsum = make_target(row_source, left, features, right, enc_gain, enc_bias, line)
-    two = [turn(three[:128], SECOND, 1), turn(one[128:], SECOND, -1)]
-    mine = [one, three, line]
+    close = near_part(active, proj_bias, [line, other_line], 0, line)
+    mine = list(gate((two, one, three), (close, tsum)))
     other = [shift(piece, "c", 1) for piece in mine]
-    close = near_part(active, proj_bias, mine, 512, one)
-    close = near_part(active, close, other, 1280, one)
-    two = list(gate(two, (close, tsum)))
-    other_two = [shift(piece, "c", 1) for piece in two]
-    grad = out_grads(timesteps, close, active, target, tsum, two + other_two)
+    close = near_part(active, close, mine[1:] + mine[:1], 512, line)
+    close = near_part(active, close, other[1:], 1280, line)
+    grad = out_grads(timesteps, close, active, target, tsum, other[:1])
+    mine, other = mine + [line], other + [other_line]
     (away_far,) = outer(rows, grad, 1024, 256, ((0, 256, bf16),))
     back_far = shift(away_far, "c", 1)
     (away,) = outer(rows, grad, 1280, 768, ((0, 768, bf16),), after=away_far)
@@ -416,15 +415,15 @@
     (far,) = outer(rows, grad, 0, 256, ((0, 256, bf16),), back_far, after=away)
     kept_outs = ((0, 256, bf16), (256, 256, bf16), (512, 256, f32))
     to_one, to_three, own = outer(rows, grad, 256, 768, kept_outs, back, after=far)
-    weight = whole_weight(two + mine + other_two + other, to_one)
-    pre_grad = pre_grads(grad, weight, pre, 0, 1536, to_three)
-    (own,) = gate((own,), (pre_grad,))
+    weight = whole_weight(mine + other, to_one)
+    pre_grad, token = pre_grads(grad, weight, pre, 0, 3, to_three)
+    (own,) = gate((own,), (token,))
     own = summed(own, (to_one, to_three, far), SECOND)
     blocks = {first: own[k * 64 : k * 64 + 64] for k, first in enumerate(LINE)}
-    block = summed(blocks[0], [blocks[d].astype(bf16) for d in (1, 3, 2)], FIRST).astype(bf16)
+    pre_grad, token = pre_grads(grad, weight, pre, 3, 1, own, pre_grad)
+    (kept,) = gate((blocks[0],), (token,))
+    block = summed(kept, [blocks[d].astype(bf16) for d in (1, 3, 2)], FIRST).astype(bf16)
     parts = lax.all_to_all(block, "z", 0, 0, tiled=True)
-    pre_grad = pre_grads(grad, weight, pre, 1536, 512, block, pre_grad)
-    (parts,) = gate((parts,), (pre_grad,))
     total = jnp.sum(parts.reshape(8, 8, width).astype(f32), axis=0).astype(bf16)
     total = jnp.broadcast_to(total[None], (8, 8, width)).reshape(block.shape)
     weight_grad = lax.all_to_all(total, "z", 0, 0, tiled=True).astype(f32)

time: 118 us -> 112 us (0.949)
  blocking collectives: 14.2 us -> 30.2 us
  local copies, waits for them, and re-layouts: 10.5 us -> 2.06 us
  waiting for transfers between devices: 27.6 us -> 21 us
  starting transfers between devices: 30.3 us -> 25.6 us
    all_to_all x0 -> x1, blocking collectives: none -> 18 us  [body(): parts = lax.all_to_all(block, 'z', 0, 0, tiled=True)]
    unnamed x28 -> x18, local copies, waits for them, and re-layouts: 10.4 us -> 1.92 us
    all_to_all x1 -> x0, starting transfers between devices: 6.58 us -> none  [body(): parts = lax.all_to_all(block, 'z', 0, 0, tiled=True)]
    ppermute x9 -> x8, waiting for transfers between devices: 11.4 us -> 7.79 us  [shift(): lax.ppermute(block, axis, [(i, (i + step) % count) for i in range(count)])]
    all_to_all x1 -> x0, waiting for transfers between devices: 2.58 us -> none  [body(): parts = lax.all_to_all(block, 'z', 0, 0, tiled=True)]
    all_to_all x1, blocking collectives: 14.2 us -> 12.2 us  [body(): weight_grad = lax.all_to_all(total, 'z', 0, 0, tiled=True).astype(f32)]
    ppermute x9 -> x8, starting transfers between devices: 5.93 us -> 7.29 us  [shift(): lax.ppermute(block, axis, [(i, (i + step) % count) for i in range(count)])]
    pallas_call x1, Pallas kernels: 4.45 us -> 3.21 us  [out_grads(): pl.pallas_call(grad_kernel, in_specs=[smem] + [whole] * 4 + [pl.BlockSpec...]
  transfers between devices with their start and end apart: 23 -> 20, of which waited for: 11 -> 10; matrix products, arithmetic and copies ran while one was open for 0% -> 0% of each run, Pallas kernels for 22% -> 24%
where the time goes in v1:
time: 112 us
  Pallas kernels  30.6 us (27%)
  blocking collectives  30.2 us (27%)
  starting transfers between devices  25.6 us (23%)
  waiting for transfers between devices  21 us (19%)
  local copies, waits for them, and re-layouts  2.06 us (2%)
  other arithmetic  1.38 us (1%)
    ppermute x12, starting transfers between devices, turn(): return lax.ppermute(block, ('y', 'x', 'c'), pairs)  18.3 us
    all_to_all x1, blocking collectives, body(): parts = lax.all_to_all(block, 'z', 0, 0, tiled=True)  18 us
    ppermute x12, waiting for transfers between devices, turn(): return lax.ppermute(block, ('y', 'x', 'c'), pairs)  13.2 us
    all_to_all x1, blocking collectives, body(): weight_grad = lax.all_to_all(total, 'z', 0, 0, tiled=True).astype(f32)  12.2 us
    pallas_call x2, Pallas kernels, pre_grads(): pl.pallas_call(pre_kernel, grid=(count,), in_specs=[pl.BlockSpec((tokens,...  8.64 us
    ppermute x8, waiting for transfers between devices, shift(): lax.ppermute(block, axis, [(i, (i + step) % count) for i in range(count)])  7.79 us
    ppermute x8, starting transfers between devices, shift(): lax.ppermute(block, axis, [(i, (i + step) % count) for i in range(count)])  7.29 us
    pallas_call x4, Pallas kernels, outer(): pl.pallas_call(functools.partial(outer_kernel, start, count // 256, outs,...  5.53 us
  transfers between devices with their start and end apart: 20, of which 10 were waited for; matrix products, arithmetic and copies ran while one was open for 0% of the time, Pallas kernels for 24%

profile of v1, /device:TPU:6, one launch (start us, length us, event | category | flops | bytes accessed | tf_op | source)
XLA Modules:
  0.0 111.8 jit_solution(7723952307648975831)
XLA Ops:
  1.5 2.4 %collective-permute-start = (bf16[64,1536]{1,0:T(8,128)(2,1)}, bf16[64,1536]{1,0:T(8,128)(2,1)S(1)}, u32[]{:S(2)}, u32[]{:S(2)}) collective-permute-start(bf16[64,1536]{1,0:T(8,128)(2,1)} %own_ref.1), channel_id=1, source_target_pairs={{0,16},{8,72},{16,32},{24,88},{32,48},{40,104},{48,0},{56,120},{64... | collective-permute-start | bytes 589832 | tf_op jit(solution)/shard_map/ppermute | solution.py:31
  4.4 1.9 %copy-done = bf16[2,6,64,2048]{3,2,1,0:T(8,128)(2,1)S(1)} copy-done((bf16[2,6,64,2048]{3,2,1,0:T(8,128)(2,1)S(1)}, bf16[2,6,64,2048]{3,2,1,0:T(8,128)(2,1)}, u32[]{:S(2)}) %copy-start) | copy-done | bytes 3145752
  6.3 4.0 %hidden_rows.1 = (bf16[2048,768]{1,0:T(8,128)(2,1)S(1)}, bf16[768,2048]{1,0:T(8,128)(2,1)S(1)}) custom-call(bf16[768,2048]{1,0:T(8,128)(2,1)S(1)} %bitcast.7), custom_call_target="tpu_custom_call" | custom-call | flops 196608 | bytes 147456 | tf_op jit(solution)/shard_map/hidden_rows/pallas_call | solution.py:118
  10.3 1.1 collective-permute-done.2.far_ref
  11.6 1.5 %collective-permute-start.6 = (bf16[256,1536]{1,0:T(8,128)(2,1)S(1)}, bf16[256,1536]{1,0:T(8,128)(2,1)S(1)}, u32[]{:S(2)}, u32[]{:S(2)}) collective-permute-start(bf16[256,1536]{1,0:T(8,128)(2,1)S(1)} %pack.1.refs_0_.refs_2_.after_ref.refs_3_), channel_id=1, source_target_pairs={{0,64},{8,24},{16,80},{24,40},{32,96},{40,56},{48,112},{56,8},{64,... | collective-permute-start | bytes 2359304 | tf_op jit(solution)/shard_map/ppermute | solution.py:31
  13.2 1.7 %collective-permute-start.5 = (bf16[256,1536]{1,0:T(8,128)(2,1)S(1)}, bf16[256,1536]{1,0:T(8,128)(2,1)S(1)}, u32[]{:S(2)}, u32[]{:S(2)}) collective-permute-start(bf16[256,1536]{1,0:T(8,128)(2,1)S(1)} %pack.1.refs_0_.refs_2_.after_ref.refs_3_), channel_id=1, source_target_pairs={{0,192},{8,56},{16,208},{24,8},{32,224},{40,24},{48,240},{56,40},{... | collective-permute-start | bytes 2359304 | tf_op jit(solution)/shard_map/ppermute | solution.py:31
  14.9 1.9 %collective-permute-start.4 = (bf16[256,1536]{1,0:T(8,128)(2,1)S(1)}, bf16[256,1536]{1,0:T(8,128)(2,1)S(1)}, u32[]{:S(2)}, u32[]{:S(2)}) collective-permute-start(bf16[256,1536]{1,0:T(8,128)(2,1)S(1)} %pack.1.refs_0_.refs_2_.after_ref.refs_3_), channel_id=1, source_target_pairs={{0,128},{8,40},{16,144},{24,56},{32,160},{40,8},{48,176},{56,24},{... | collective-permute-start | bytes 2359304 | tf_op jit(solution)/shard_map/ppermute | solution.py:31
  16.9 2.0 %collective-permute-start.7 = (bf16[2,2,32,1536]{3,2,1,0:T(8,128)(2,1)S(1)}, bf16[2,2,32,1536]{3,2,1,0:T(8,128)(2,1)S(1)}, u32[]{:S(2)}, u32[]{:S(2)}) collective-permute-start(bf16[2,2,32,1536]{3,2,1,0:T(8,128)(2,1)S(1)} %get-tuple-element.20), channel_id=1, source_target_pairs={{0,1},{1,2},{2,3},{3,4},{4,5},{5,6},{6,7},{7,0},{8,9},{9,10},{10,1... | collective-permute-start | bytes 1179656 | tf_op jit(solution)/shard_map/ppermute | solution.py:20
  18.9 4.0 %collective-permute-start.8 = (bf16[2,2,32,1536]{3,2,1,0:T(8,128)(2,1)S(1)}, bf16[2,2,32,1536]{3,2,1,0:T(8,128)(2,1)S(1)}, u32[]{:S(2)}, u32[]{:S(2)}) collective-permute-start(bf16[2,2,32,1536]{3,2,1,0:T(8,128)(2,1)S(1)} %get-tuple-element.21), channel_id=1, source_target_pairs={{0,7},{1,0},{2,1},{3,2},{4,3},{5,4},{6,5},{7,6},{8,15},{9,8},{10,9... | collective-permute-start | bytes 1179656 | tf_op jit(solution)/shard_map/ppermute | solution.py:20
  22.9 1.5 %near_part.3.refs_3_.base_ref = f32[768,1536]{1,0:T(8,128)S(1)} custom-call(bf16[768,2048]{1,0:T(8,128)(2,1)S(1)} %get-tuple-element.18.act_ref, f32[1536]{0:T(1024)S(1)} %copy-done.6, bf16[256,1536]{1,0:T(8,128)(2,1)S(1)} %pack.1.refs_0_.refs_2_.after_ref.refs_3_, bf16[256,1536]{1,0:T(8,128)(2,1)S(1)} %collective-permute-done.3.refs_1_.refs_2_.refs_7_, ...), custom_call_target="tpu_custom_call" | custom-call | flops 28311552 | bytes 131072 | tf_op jit(solution)/shard_map/near_part/pallas_call | solution.py:204
  24.5 6.1 %collective-permute-done.7.left_ref = bf16[2,2,32,1536]{3,2,1,0:T(8,128)(2,1)S(1)} collective-permute-done((bf16[2,2,32,1536]{3,2,1,0:T(8,128)(2,1)S(1)}, bf16[2,2,32,1536]{3,2,1,0:T(8,128)(2,1)S(1)}, u32[]{:S(2)}, u32[]{:S(2)}) %collective-permute-start.7) | collective-permute-done | bytes 393248 | tf_op jit(solution)/shard_map/ppermute | solution.py:20
  30.6 2.9 %make_target.1 = (f32[768,1536]{1,0:T(8,128)S(1)}, f32[768,128]{1,0:T(8,128)S(1)}) custom-call(s32[2,6]{1,0:T(2,128)S(1)} %copy-done.7, bf16[2,2,32,1536]{3,2,1,0:T(8,128)(2,1)S(1)} %collective-permute-done.7.left_ref, bf16[2,3,32,1536]{3,2,1,0:T(8,128)(2,1)S(1)} %copy-done.2, bf16[2,2,32,1536]{3,2,1,0:T(8,128)(2,1)S(1)} %collective-permute-done.8.right_ref, ...), custom_call_target="tpu_custom_call" | custom-call | flops 8257536 | bytes 147456 | tf_op jit(solution)/shard_map/make_target/pallas_call | solution.py:170
  33.5 0.9 collective-permute-done.4.refs_0_
  35.0 2.2 %near_part.4.base_ref = f32[768,1536]{1,0:T(8,128)S(1)} custom-call(bf16[768,2048]{1,0:T(8,128)(2,1)S(1)} %get-tuple-element.18.act_ref, f32[768,1536]{1,0:T(8,128)S(1)} %near_part.3.refs_3_.base_ref, bf16[256,1536]{1,0:T(8,128)(2,1)S(1)} %get-tuple-element.23.refs_0_.refs_1_, bf16[256,1536]{1,0:T(8,128)(2,1)S(1)} %get-tuple-element.24.refs_1_.refs_2_, ...), custom_call_target="tpu_custom_call" | custom-call | flops 28311552 | bytes 131072 | tf_op jit(solution)/shard_map/near_part/pallas_call | solution.py:204
  37.9 1.5 %near_part.5.near_ref = f32[768,1536]{1,0:T(8,128)S(1)} custom-call(bf16[768,2048]{1,0:T(8,128)(2,1)S(1)} %get-tuple-element.18.act_ref, f32[768,1536]{1,0:T(8,128)S(1)} %near_part.4.base_ref, bf16[256,1536]{1,0:T(8,128)(2,1)S(1)} %collective-permute-done.9.refs_0_.refs_5_, bf16[256,1536]{1,0:T(8,128)(2,1)S(1)} %collective-permute-done.10.refs_1_.refs_6_, ...), custom_call_target="tpu_custom_call" | custom-call | flops 28311552 | bytes 131072 | tf_op jit(solution)/shard_map/near_part/pallas_call | solution.py:204
  39.4 3.2 %out_grads.1.refs_1_.grad_ref = bf16[768,1536]{1,0:T(8,128)(2,1)S(1)} custom-call(s32[2]{0:T(128)S(1)} %copy-done.8, f32[768,1536]{1,0:T(8,128)S(1)} %near_part.5.near_ref, bf16[768,2048]{1,0:T(8,128)(2,1)S(1)} %get-tuple-element.18.act_ref, f32[768,1536]{1,0:T(8,128)S(1)} %get-tuple-element.26.target_ref, ...), custom_call_target="tpu_custom_call" | custom-call | flops 18874368 | bytes 245760 | tf_op jit(solution)/shard_map/out_grads/pallas_call | solution.py:257
  43.7 2.0 %outer.5.refs_0_ = bf16[768,1536]{1,0:T(8,128)(2,1)S(1)} custom-call(bf16[2048,768]{1,0:T(8,128)(2,1)S(1)} %get-tuple-element.19.after_ref.refs_0_, bf16[768,1536]{1,0:T(8,128)(2,1)S(1)} %out_grads.1.refs_1_.grad_ref, bf16[256,1536]{1,0:T(8,128)(2,1)S(1)} %outer.4.refs_2_), custom_call_target="tpu_custom_call" | custom-call | flops 28311552 | bytes 65536 | tf_op jit(solution)/shard_map/outer/pallas_call | solution.py:297
  46.9 2.5 %collective-permute-start.16 = (bf16[256,1536]{1,0:T(8,128)(2,1)S(1)}, bf16[256,1536]{1,0:T(8,128)(2,1)S(1)}, u32[]{:S(2)}, u32[]{:S(2)}) collective-permute-start(bf16[256,1536]{1,0:T(8,128)(2,1)S(1)} %outer.6.refs_3_), channel_id=1, source_target_pairs={{0,128},{8,40},{16,144},{24,56},{32,160},{40,8},{48,176},{56,24},{... | collective-permute-start | bytes 2359304 | tf_op jit(solution)/shard_map/ppermute | solution.py:31
  50.3 2.0 %outer.7 = (bf16[256,1536]{1,0:T(8,128)(2,1)S(1)}, bf16[256,1536]{1,0:T(8,128)(2,1)S(1)}, f32[256,1536]{1,0:T(8,128)S(1)}) custom-call(bf16[2048,768]{1,0:T(8,128)(2,1)S(1)} %get-tuple-element.19.after_ref.refs_0_, bf16[768,1536]{1,0:T(8,128)(2,1)S(1)} %out_grads.1.refs_1_.grad_ref, bf16[768,1536]{1,0:T(8,128)(2,1)S(1)} %collective-permute-done.13.refs_2_, ...), custom_call_target="tpu_custom_call" | custom-call | flops 28311552 | bytes 65536 | tf_op jit(solution)/shard_map/outer/pallas_call | solution.py:297
  52.3 1.5 %collective-permute-start.14 = (bf16[256,1536]{1,0:T(8,128)(2,1)S(1)}, bf16[256,1536]{1,0:T(8,128)(2,1)S(1)}, u32[]{:S(2)}, u32[]{:S(2)}) collective-permute-start(bf16[256,1536]{1,0:T(8,128)(2,1)S(1)} %get-tuple-element.27.refs_8_), channel_id=1, source_target_pairs={{0,64},{8,24},{16,80},{24,40},{32,96},{40,56},{48,112},{56,8},{64,... | collective-permute-start | bytes 2359304 | tf_op jit(solution)/shard_map/ppermute | solution.py:31
  53.8 1.8 %collective-permute-start.15 = (bf16[256,1536]{1,0:T(8,128)(2,1)S(1)}, bf16[256,1536]{1,0:T(8,128)(2,1)S(1)}, u32[]{:S(2)}, u32[]{:S(2)}) collective-permute-start(bf16[256,1536]{1,0:T(8,128)(2,1)S(1)} %get-tuple-element.29.refs_0_), channel_id=1, source_target_pairs={{0,192},{8,56},{16,208},{24,8},{32,224},{40,24},{48,240},{56,40},{... | collective-permute-start | bytes 2359304 | tf_op jit(solution)/shard_map/ppermute | solution.py:31
  55.6 1.0 whole_weight.1.w_ref
  56.7 6.1 %pre_grads.2 = (bf16[768,2048]{1,0:T(8,128)(2,1)}, f32[8,128]{1,0:T(8,128)S(1)}) custom-call(bf16[768,1536]{1,0:T(8,128)(2,1)S(1)} %out_grads.1.refs_1_.grad_ref, bf16[2048,1536]{1,0:T(8,128)(2,1)S(1)} %whole_weight.1.w_ref, bf16[768,2048]{1,0:T(8,128)(2,1)S(1)} %bitcast.8, bf16[256,1536]{1,0:T(8,128)(2,1)S(1)} %get-tuple-element.29.refs_0_), custom_call_target="tpu_custom_call" | custom-call | flops 56623104 | bytes 196608 | tf_op jit(solution)/shard_map/pre_grads/pallas_call | solution.py:364
  62.8 6.1 %collective-permute-done.14 = bf16[256,1536]{1,0:T(8,128)(2,1)S(1)} collective-permute-done((bf16[256,1536]{1,0:T(8,128)(2,1)S(1)}, bf16[256,1536]{1,0:T(8,128)(2,1)S(1)}, u32[]{:S(2)}, u32[]{:S(2)}) %collective-permute-start.14) | collective-permute-done | bytes 786464 | tf_op jit(solution)/shard_map/ppermute | solution.py:31
  69.5 1.9 %collective-permute-start.17 = (bf16[64,1536]{1,0:T(8,128)(2,1)S(1)}, bf16[64,1536]{1,0:T(8,128)(2,1)S(1)}, u32[]{:S(2)}, u32[]{:S(2)}) collective-permute-start(bf16[64,1536]{1,0:T(8,128)(2,1)S(1)} %get-tuple-element.36), channel_id=1, source_target_pairs={{0,16},{8,72},{16,32},{24,88},{32,48},{40,104},{48,0},{56,120},{64... | collective-permute-start | bytes 589832 | tf_op jit(solution)/shard_map/ppermute | solution.py:31
  71.4 1.2 %collective-permute-start.19 = (bf16[64,1536]{1,0:T(8,128)(2,1)S(1)}, bf16[64,1536]{1,0:T(8,128)(2,1)S(1)}, u32[]{:S(2)}, u32[]{:S(2)}) collective-permute-start(bf16[64,1536]{1,0:T(8,128)(2,1)S(1)} %get-tuple-element.37), channel_id=1, source_target_pairs={{0,32},{8,136},{16,48},{24,152},{32,0},{40,168},{48,16},{56,184},{... | collective-permute-start | bytes 589832 | tf_op jit(solution)/shard_map/ppermute | solution.py:31
  73.1 2.5 %pre_grads.3 = (bf16[768,2048]{1,0:T(8,128)(2,1)}, f32[8,128]{1,0:T(8,128)S(1)}) custom-call(bf16[768,1536]{1,0:T(8,128)(2,1)S(1)} %out_grads.1.refs_1_.grad_ref, bf16[2048,1536]{1,0:T(8,128)(2,1)S(1)} %whole_weight.1.w_ref, bf16[768,2048]{1,0:T(8,128)(2,1)S(1)} %bitcast.9, ...), custom_call_target="tpu_custom_call", output_to_operand_aliasing={{0}: (4, {})} | custom-call | flops 18874368 | bytes 65536 | tf_op jit(solution)/shard_map/pre_grads/pallas_call | solution.py:364
  75.6 1.1 collective-permute-done.17
  76.7 1.9 %collective-permute-done.19 = bf16[64,1536]{1,0:T(8,128)(2,1)S(1)} collective-permute-done((bf16[64,1536]{1,0:T(8,128)(2,1)S(1)}, bf16[64,1536]{1,0:T(8,128)(2,1)S(1)}, u32[]{:S(2)}, u32[]{:S(2)}) %collective-permute-start.19) | collective-permute-done | bytes 196640 | tf_op jit(solution)/shard_map/ppermute | solution.py:31
  78.7 2.0 %collective-permute-done.18 = bf16[64,1536]{1,0:T(8,128)(2,1)S(1)} collective-permute-done((bf16[64,1536]{1,0:T(8,128)(2,1)S(1)}, bf16[64,1536]{1,0:T(8,128)(2,1)S(1)}, u32[]{:S(2)}, u32[]{:S(2)}) %collective-permute-start.18) | collective-permute-done | bytes 196640 | tf_op jit(solution)/shard_map/ppermute | solution.py:31
  80.8 18.0 %all_to_all.15 = bf16[8,8,1536]{2,1,0:T(8,128)(2,1)S(1)} all-to-all(bf16[8,8,1536]{2,1,0:T(8,128)(2,1)S(1)} %fusion), channel_id=1, replica_groups=mesh['y'=4,'x'=4,'c'=2,'z'=8] {'z'}, dimensions={0} | all-to-all | bytes 393216 | tf_op jit(solution)/shard_map/all_to_all | solution.py:426
  98.8 12.2 %all_to_all.16 = bf16[8,8,1536]{2,1,0:T(8,128)(2,1)S(1)} all-to-all(bf16[8,8,1536]{2,1,0:T(8,128)(2,1)S(1)} %broadcast_in_dim.2), channel_id=1, replica_groups=mesh['y'=4,'x'=4,'c'=2,'z'=8] {'z'}, dimensions={0} | all-to-all | bytes 393216 | tf_op jit(solution)/shard_map/all_to_all | solution.py:429
  (55 shorter events, 7.9 us)
Async XLA Ops:
  0.6 9.6 %collective-permute-start.1 = (bf16[64,1536]{1,0:T(8,128)(2,1)}, bf16[64,1536]{1,0:T(8,128)(2,1)S(1)}, u32[]{:S(2)}, u32[]{:S(2)}) collective-permute-start(bf16[64,1536]{1,0:T(8,128)(2,1)} %own_ref.1), channel_id=1, source_target_pairs={{0,48},{8,200},{16,0},{24,216},{32,16},{40,232},{48,32},{56,248},{... | collective-permute-start | bytes 589832 | tf_op jit(solution)/shard_map/ppermute | solution.py:31
  1.5 8.7 %collective-permute-start = (bf16[64,1536]{1,0:T(8,128)(2,1)}, bf16[64,1536]{1,0:T(8,128)(2,1)S(1)}, u32[]{:S(2)}, u32[]{:S(2)}) collective-permute-start(bf16[64,1536]{1,0:T(8,128)(2,1)} %own_ref.1), channel_id=1, source_target_pairs={{0,16},{8,72},{16,32},{24,88},{32,48},{40,104},{48,0},{56,120},{64... | collective-permute-start | bytes 589832 | tf_op jit(solution)/shard_map/ppermute | solution.py:31
  3.9 7.4 %collective-permute-start.2 = (bf16[64,1536]{1,0:T(8,128)(2,1)}, bf16[64,1536]{1,0:T(8,128)(2,1)S(1)}, u32[]{:S(2)}, u32[]{:S(2)}) collective-permute-start(bf16[64,1536]{1,0:T(8,128)(2,1)} %own_ref.1), channel_id=1, source_target_pairs={{0,32},{8,136},{16,48},{24,152},{32,0},{40,168},{48,16},{56,184},{... | collective-permute-start | bytes 589832 | tf_op jit(solution)/shard_map/ppermute | solution.py:31
  4.4 1.9 %copy-start = (bf16[2,6,64,2048]{3,2,1,0:T(8,128)(2,1)S(1)}, bf16[2,6,64,2048]{3,2,1,0:T(8,128)(2,1)}, u32[]{:S(2)}) copy-start(bf16[2,6,64,2048]{3,2,1,0:T(8,128)(2,1)} %param.13) | copy-start | bytes 9437188
  6.3 5.1 %copy-start.3 = (bf16[64,1536]{1,0:T(8,128)(2,1)S(1)}, bf16[64,1536]{1,0:T(8,128)(2,1)}, u32[]{:S(2)}) copy-start(bf16[64,1536]{1,0:T(8,128)(2,1)} %own_ref.1) | copy-start | bytes 589828
  11.3 5.5 %copy-start.2 = (bf16[2,3,32,1536]{3,2,1,0:T(8,128)(2,1)S(1)}, bf16[2,3,32,1536]{3,2,1,0:T(8,128)(2,1)}, u32[]{:S(2)}) copy-start(bf16[2,3,32,1536]{3,2,1,0:T(8,128)(2,1)} %mid_ref.1) | copy-start | bytes 1769476
  11.4 11.5 %copy-start.6 = (f32[1536]{0:T(1024)S(1)}, f32[1536]{0:T(1024)}, u32[]{:S(2)}) copy-start(f32[1536]{0:T(1024)} %base_ref.1) | copy-start | bytes 18436
  11.4 5.5 %collective-permute-start.3 = (bf16[256,1536]{1,0:T(8,128)(2,1)S(1)}, bf16[256,1536]{1,0:T(8,128)(2,1)S(1)}, u32[]{:S(2)}, u32[]{:S(2)}) collective-permute-start(bf16[256,1536]{1,0:T(8,128)(2,1)S(1)} %pack.1.refs_0_.refs_2_.after_ref.refs_3_), channel_id=1, source_target_pairs={{0,8},{8,0},{1,9},{9,1},{2,10},{10,2},{3,11},{11,3},{4,12},{12,4},... | collective-permute-start | bytes 2359304 | tf_op jit(solution)/shard_map/ppermute | solution.py:20
  11.6 21.9 %collective-permute-start.6 = (bf16[256,1536]{1,0:T(8,128)(2,1)S(1)}, bf16[256,1536]{1,0:T(8,128)(2,1)S(1)}, u32[]{:S(2)}, u32[]{:S(2)}) collective-permute-start(bf16[256,1536]{1,0:T(8,128)(2,1)S(1)} %pack.1.refs_0_.refs_2_.after_ref.refs_3_), channel_id=1, source_target_pairs={{0,64},{8,24},{16,80},{24,40},{32,96},{40,56},{48,112},{56,8},{64,... | collective-permute-start | bytes 2359304 | tf_op jit(solution)/shard_map/ppermute | solution.py:31
  13.2 20.3 %collective-permute-start.5 = (bf16[256,1536]{1,0:T(8,128)(2,1)S(1)}, bf16[256,1536]{1,0:T(8,128)(2,1)S(1)}, u32[]{:S(2)}, u32[]{:S(2)}) collective-permute-start(bf16[256,1536]{1,0:T(8,128)(2,1)S(1)} %pack.1.refs_0_.refs_2_.after_ref.refs_3_), channel_id=1, source_target_pairs={{0,192},{8,56},{16,208},{24,8},{32,224},{40,24},{48,240},{56,40},{... | collective-permute-start | bytes 2359304 | tf_op jit(solution)/shard_map/ppermute | solution.py:31
  14.9 19.6 %collective-permute-start.4 = (bf16[256,1536]{1,0:T(8,128)(2,1)S(1)}, bf16[256,1536]{1,0:T(8,128)(2,1)S(1)}, u32[]{:S(2)}, u32[]{:S(2)}) collective-permute-start(bf16[256,1536]{1,0:T(8,128)(2,1)S(1)} %pack.1.refs_0_.refs_2_.after_ref.refs_3_), channel_id=1, source_target_pairs={{0,128},{8,40},{16,144},{24,56},{32,160},{40,8},{48,176},{56,24},{... | collective-permute-start | bytes 2359304 | tf_op jit(solution)/shard_map/ppermute | solution.py:31
  16.9 13.7 %collective-permute-start.7 = (bf16[2,2,32,1536]{3,2,1,0:T(8,128)(2,1)S(1)}, bf16[2,2,32,1536]{3,2,1,0:T(8,128)(2,1)S(1)}, u32[]{:S(2)}, u32[]{:S(2)}) collective-permute-start(bf16[2,2,32,1536]{3,2,1,0:T(8,128)(2,1)S(1)} %get-tuple-element.20), channel_id=1, source_target_pairs={{0,1},{1,2},{2,3},{3,4},{4,5},{5,6},{6,7},{7,0},{8,9},{9,10},{10,1... | collective-permute-start | bytes 1179656 | tf_op jit(solution)/shard_map/ppermute | solution.py:20
  18.9 11.7 %collective-permute-start.8 = (bf16[2,2,32,1536]{3,2,1,0:T(8,128)(2,1)S(1)}, bf16[2,2,32,1536]{3,2,1,0:T(8,128)(2,1)S(1)}, u32[]{:S(2)}, u32[]{:S(2)}) collective-permute-start(bf16[2,2,32,1536]{3,2,1,0:T(8,128)(2,1)S(1)} %get-tuple-element.21), channel_id=1, source_target_pairs={{0,7},{1,0},{2,1},{3,2},{4,3},{5,4},{6,5},{7,6},{8,15},{9,8},{10,9... | collective-permute-start | bytes 1179656 | tf_op jit(solution)/shard_map/ppermute | solution.py:20
  22.9 7.6 %copy-start.4 = (f32[1536]{0:T(1024)S(1)}, f32[1536]{0:T(1024)}, u32[]{:S(2)}) copy-start(f32[1536]{0:T(1024)} %gain_ref.1) | copy-start | bytes 18436
  22.9 7.6 %copy-start.5 = (f32[1536]{0:T(1024)S(1)}, f32[1536]{0:T(1024)}, u32[]{:S(2)}) copy-start(f32[1536]{0:T(1024)} %bias_ref.1) | copy-start | bytes 18436
  22.9 7.6 %copy-start.7 = (s32[2,6]{1,0:T(2,128)S(1)}, s32[2,6]{1,0:T(2,128)}, u32[]{:S(2)}) copy-start(s32[2,6]{1,0:T(2,128)} %source_ref.1) | copy-start | bytes 148
  34.4 2.7 %collective-permute-start.9 = (bf16[256,1536]{1,0:T(8,128)(2,1)S(1)}, bf16[256,1536]{1,0:T(8,128)(2,1)S(1)}, u32[]{:S(2)}, u32[]{:S(2)}) collective-permute-start(bf16[256,1536]{1,0:T(8,128)(2,1)S(1)} %get-tuple-element.23.refs_0_.refs_1_), channel_id=1, source_target_pairs={{0,8},{8,0},{1,9},{9,1},{2,10},{10,2},{3,11},{11,3},{4,12},{12,4},... | collective-permute-start | bytes 2359304 | tf_op jit(solution)/shard_map/ppermute | solution.py:20
  34.5 3.4 %collective-permute-start.10 = (bf16[256,1536]{1,0:T(8,128)(2,1)S(1)}, bf16[256,1536]{1,0:T(8,128)(2,1)S(1)}, u32[]{:S(2)}, u32[]{:S(2)}) collective-permute-start(bf16[256,1536]{1,0:T(8,128)(2,1)S(1)} %get-tuple-element.24.refs_1_.refs_2_), channel_id=1, source_target_pairs={{0,8},{8,0},{1,9},{9,1},{2,10},{10,2},{3,11},{11,3},{4,12},{12,4},... | collective-permute-start | bytes 2359304 | tf_op jit(solution)/shard_map/ppermute | solution.py:20
  35.0 4.5 %collective-permute-start.11 = (bf16[256,1536]{1,0:T(8,128)(2,1)S(1)}, bf16[256,1536]{1,0:T(8,128)(2,1)S(1)}, u32[]{:S(2)}, u32[]{:S(2)}) collective-permute-start(bf16[256,1536]{1,0:T(8,128)(2,1)S(1)} %get-tuple-element.25.refs_2_.refs_0_), channel_id=1, source_target_pairs={{0,8},{8,0},{1,9},{9,1},{2,10},{10,2},{3,11},{11,3},{4,12},{12,4},... | collective-permute-start | bytes 2359304 | tf_op jit(solution)/shard_map/ppermute | solution.py:20
  37.2 2.2 %copy-start.8 = (s32[2]{0:T(128)S(1)}, s32[2]{0:T(128)}, u32[]{:S(2)}) copy-start(s32[2]{0:T(128)} %time_ref.1) | copy-start | bytes 28
  43.4 2.4 %collective-permute-start.12 = (bf16[256,1536]{1,0:T(8,128)(2,1)S(1)}, bf16[256,1536]{1,0:T(8,128)(2,1)S(1)}, u32[]{:S(2)}, u32[]{:S(2)}) collective-permute-start(bf16[256,1536]{1,0:T(8,128)(2,1)S(1)} %outer.4.refs_2_), channel_id=1, source_target_pairs={{0,8},{8,0},{1,9},{9,1},{2,10},{10,2},{3,11},{11,3},{4,12},{12,4},... | collective-permute-start | bytes 2359304 | tf_op jit(solution)/shard_map/ppermute | solution.py:20
  45.8 4.5 %collective-permute-start.13 = (bf16[768,1536]{1,0:T(8,128)(2,1)S(1)}, bf16[768,1536]{1,0:T(8,128)(2,1)S(1)}, u32[]{:S(2)}, u32[]{:S(2)}) collective-permute-start(bf16[768,1536]{1,0:T(8,128)(2,1)S(1)} %gate.7.refs_3_), channel_id=1, source_target_pairs={{0,8},{8,0},{1,9},{9,1},{2,10},{10,2},{3,11},{11,3},{4,12},{12,4},... | collective-permute-start | bytes 7077896 | tf_op jit(solution)/shard_map/ppermute | solution.py:20
  46.9 15.9 %collective-permute-start.16 = (bf16[256,1536]{1,0:T(8,128)(2,1)S(1)}, bf16[256,1536]{1,0:T(8,128)(2,1)S(1)}, u32[]{:S(2)}, u32[]{:S(2)}) collective-permute-start(bf16[256,1536]{1,0:T(8,128)(2,1)S(1)} %outer.6.refs_3_), channel_id=1, source_target_pairs={{0,128},{8,40},{16,144},{24,56},{32,160},{40,8},{48,176},{56,24},{... | collective-permute-start | bytes 2359304 | tf_op jit(solution)/shard_map/ppermute | solution.py:31
  52.3 16.6 %collective-permute-start.14 = (bf16[256,1536]{1,0:T(8,128)(2,1)S(1)}, bf16[256,1536]{1,0:T(8,128)(2,1)S(1)}, u32[]{:S(2)}, u32[]{:S(2)}) collective-permute-start(bf16[256,1536]{1,0:T(8,128)(2,1)S(1)} %get-tuple-element.27.refs_8_), channel_id=1, source_target_pairs={{0,64},{8,24},{16,80},{24,40},{32,96},{40,56},{48,112},{56,8},{64,... | collective-permute-start | bytes 2359304 | tf_op jit(solution)/shard_map/ppermute | solution.py:31
  53.8 2.9 %copy-start.1 = (bf16[2,6,64,2048]{3,2,1,0:T(8,128)(2,1)S(1)}, bf16[2,6,64,2048]{3,2,1,0:T(8,128)(2,1)}, u32[]{:S(2)}) copy-start(bf16[2,6,64,2048]{3,2,1,0:T(8,128)(2,1)} %param.13) | copy-start | bytes 9437188
  53.8 15.1 %collective-permute-start.15 = (bf16[256,1536]{1,0:T(8,128)(2,1)S(1)}, bf16[256,1536]{1,0:T(8,128)(2,1)S(1)}, u32[]{:S(2)}, u32[]{:S(2)}) collective-permute-start(bf16[256,1536]{1,0:T(8,128)(2,1)S(1)} %get-tuple-element.29.refs_0_), channel_id=1, source_target_pairs={{0,192},{8,56},{16,208},{24,8},{32,224},{40,24},{48,240},{56,40},{... | collective-permute-start | bytes 2359304 | tf_op jit(solution)/shard_map/ppermute | solution.py:31
  69.5 7.2 %collective-permute-start.17 = (bf16[64,1536]{1,0:T(8,128)(2,1)S(1)}, bf16[64,1536]{1,0:T(8,128)(2,1)S(1)}, u32[]{:S(2)}, u32[]{:S(2)}) collective-permute-start(bf16[64,1536]{1,0:T(8,128)(2,1)S(1)} %get-tuple-element.36), channel_id=1, source_target_pairs={{0,16},{8,72},{16,32},{24,88},{32,48},{40,104},{48,0},{56,120},{64... | collective-permute-start | bytes 589832 | tf_op jit(solution)/shard_map/ppermute | solution.py:31
  71.4 7.3 %collective-permute-start.19 = (bf16[64,1536]{1,0:T(8,128)(2,1)S(1)}, bf16[64,1536]{1,0:T(8,128)(2,1)S(1)}, u32[]{:S(2)}, u32[]{:S(2)}) collective-permute-start(bf16[64,1536]{1,0:T(8,128)(2,1)S(1)} %get-tuple-element.37), channel_id=1, source_target_pairs={{0,32},{8,136},{16,48},{24,152},{32,0},{40,168},{48,16},{56,184},{... | collective-permute-start | bytes 589832 | tf_op jit(solution)/shard_map/ppermute | solution.py:31
  72.6 8.0 %collective-permute-start.18 = (bf16[64,1536]{1,0:T(8,128)(2,1)S(1)}, bf16[64,1536]{1,0:T(8,128)(2,1)S(1)}, u32[]{:S(2)}, u32[]{:S(2)}) collective-permute-start(bf16[64,1536]{1,0:T(8,128)(2,1)S(1)} %get-tuple-element.38), channel_id=1, source_target_pairs={{0,48},{8,200},{16,0},{24,216},{32,16},{40,232},{48,32},{56,248},{... | collective-permute-start | bytes 589832 | tf_op jit(solution)/shard_map/ppermute | solution.py:31

commit v2 on v1

--- a/solution.py
+++ b/solution.py
@@ -214,7 +214,7 @@
 
 
 def grad_kernel(time_ref, near_ref, act_ref, target_ref, tsum_ref, *refs):
-    pieces, (out_ref, proj_ref, pp_ref, pt_ref, w_ref, sem_ref) = refs[:1], refs[1:]
+    pieces, (out_ref, proj_ref, w_ref, sem_ref) = refs[:1], refs[1:]
     copies = [
         pltpu.make_async_copy(piece_ref, w_ref.at[k * 256 : k * 256 + 256], sem_ref.at[k])
         for k, piece_ref in enumerate(pieces)
@@ -224,30 +224,31 @@
     for copy in copies:
         copy.wait()
     width = out_ref.shape[1]
-    step = 256
-    pp_ref[...] = jnp.zeros_like(pp_ref)
-    pt_ref[...] = jnp.zeros_like(pt_ref)
-
-    for n in range(width // step):
-        at = slice(n * step, n * step + step)
-        proj = near_ref[:, at] + jnp.dot(act_ref[:, 1792:2048], w_ref[:, at], preferred_element_type=f32)
-        proj_ref[:, at] = proj
-        target = target_ref[:, at]
-        square, cross = proj * proj, proj * target
-        pp_ref[...] += square[:, :128] + square[:, 128:]
-        pt_ref[...] += cross[:, :128] + cross[:, 128:]
-
+    step, group = 256, 256
     half_tokens = out_ref.shape[0] // 2
-    for part in range(12):
-        rows = slice(part * 64, part * 64 + 64)
-        scaled = -loss_scale * (1.0 - time_ref[part * 64 // half_tokens].astype(f32) * 0.001)
-        pn2 = jnp.sum(pp_ref[rows, :], axis=-1, keepdims=True) + norm_eps
-        pt = jnp.sum(pt_ref[rows, :], axis=-1, keepdims=True)
-        tn2 = tsum_ref[rows, 0:1] + norm_eps
-        inv = lax.rsqrt(pn2) * lax.rsqrt(tn2)
-        near = scaled * inv
-        along = scaled * (pt * inv) / pn2
-        out_ref[rows, :] = (near * target_ref[rows, :] - along * proj_ref[rows, :]).astype(bf16)
+    for first in range(0, out_ref.shape[0], group):
+        here_rows = slice(first, first + group)
+        pp = pt = jnp.zeros((group, 128), f32)
+        for n in range(width // step):
+            at = slice(n * step, n * step + step)
+            proj = near_ref[here_rows, at] + jnp.dot(
+                act_ref[here_rows, 1792:2048], w_ref[:, at], preferred_element_type=f32
+            )
+            proj_ref[here_rows, at] = proj
+            target = target_ref[here_rows, at]
+            square, cross = proj * proj, proj * target
+            pp = pp + (square[:, :128] + square[:, 128:])
+            pt = pt + (cross[:, :128] + cross[:, 128:])
+        for part in range(0, group, 64):
+            rows = slice(first + part, first + part + 64)
+            scaled = -loss_scale * (1.0 - time_ref[(first + part) // half_tokens].astype(f32) * 0.001)
+            pn2 = jnp.sum(pp[part : part + 64], axis=-1, keepdims=True) + norm_eps
+            cross_sum = jnp.sum(pt[part : part + 64], axis=-1, keepdims=True)
+            tn2 = tsum_ref[rows, 0:1] + norm_eps
+            inv = lax.rsqrt(pn2) * lax.rsqrt(tn2)
+            near = scaled * inv
+            along = scaled * (cross_sum * inv) / pn2
+            out_ref[rows, :] = (near * target_ref[rows, :] - along * proj_ref[rows, :]).astype(bf16)
 
 
 def out_grads(timesteps, near, active, target, tsum, pieces):
@@ -261,8 +262,6 @@
         out_shape=jax.ShapeDtypeStruct((tokens, width), bf16),
         scratch_shapes=[
             pltpu.VMEM((tokens, width), f32),
-            pltpu.VMEM((tokens, 128), f32),
-            pltpu.VMEM((tokens, 128), f32),
             pltpu.VMEM((256, width), bf16),
             pltpu.SemaphoreType.DMA((1,)),
         ],

time: 112 us -> 112 us (level)
  no operation moved by 1% of the time
where the time goes in v2:
time: 112 us; the launch traced here: 111 us
  Pallas kernels  30.2 us (27%)
  blocking collectives  30.2 us (27%)
  starting transfers between devices  25.6 us (23%)
  waiting for transfers between devices  21 us (19%)
  local copies, waits for them, and re-layouts  2.06 us (2%)
  other arithmetic  1.38 us (1%)
    ppermute x12, starting transfers between devices, turn(): return lax.ppermute(block, ('y', 'x', 'c'), pairs)  18.3 us
    all_to_all x1, blocking collectives, body(): parts = lax.all_to_all(block, 'z', 0, 0, tiled=True)  18 us
    ppermute x12, waiting for transfers between devices, turn(): return lax.ppermute(block, ('y', 'x', 'c'), pairs)  13.2 us
    all_to_all x1, blocking collectives, body(): weight_grad = lax.all_to_all(total, 'z', 0, 0, tiled=True).astype(f32)  12.2 us
    pallas_call x2, Pallas kernels, pre_grads(): pl.pallas_call(pre_kernel, grid=(count,), in_specs=[pl.BlockSpec((tokens,...  8.63 us
    ppermute x8, waiting for transfers between devices, shift(): lax.ppermute(block, axis, [(i, (i + step) % count) for i in range(count)])  7.79 us
    ppermute x8, starting transfers between devices, shift(): lax.ppermute(block, axis, [(i, (i + step) % count) for i in range(count)])  7.29 us
    pallas_call x4, Pallas kernels, outer(): pl.pallas_call(functools.partial(outer_kernel, start, count // 256, outs,...  5.53 us
  transfers between devices with their start and end apart: 20, of which 10 were waited for; matrix products, arithmetic and copies ran while one was open for 0% of the time, Pallas kernels for 24%

profile of v2, /device:TPU:6, one launch (start us, length us, event | category | flops | bytes accessed | tf_op | source)
XLA Modules:
  0.0 111.4 jit_solution(10724208915505356777)
XLA Ops:
  1.5 2.4 %collective-permute-start = (bf16[64,1536]{1,0:T(8,128)(2,1)}, bf16[64,1536]{1,0:T(8,128)(2,1)S(1)}, u32[]{:S(2)}, u32[]{:S(2)}) collective-permute-start(bf16[64,1536]{1,0:T(8,128)(2,1)} %own_ref.1), channel_id=1, source_target_pairs={{0,16},{8,72},{16,32},{24,88},{32,48},{40,104},{48,0},{56,120},{64... | collective-permute-start | bytes 589832 | tf_op jit(solution)/shard_map/ppermute | solution.py:31
  4.4 1.9 %copy-done = bf16[2,6,64,2048]{3,2,1,0:T(8,128)(2,1)S(1)} copy-done((bf16[2,6,64,2048]{3,2,1,0:T(8,128)(2,1)S(1)}, bf16[2,6,64,2048]{3,2,1,0:T(8,128)(2,1)}, u32[]{:S(2)}) %copy-start) | copy-done | bytes 3145752
  6.3 4.0 %hidden_rows.1 = (bf16[2048,768]{1,0:T(8,128)(2,1)S(1)}, bf16[768,2048]{1,0:T(8,128)(2,1)S(1)}) custom-call(bf16[768,2048]{1,0:T(8,128)(2,1)S(1)} %bitcast.7), custom_call_target="tpu_custom_call" | custom-call | flops 196608 | bytes 147456 | tf_op jit(solution)/shard_map/hidden_rows/pallas_call | solution.py:118
  10.3 1.1 collective-permute-done.2.far_ref
  11.6 1.5 %collective-permute-start.6 = (bf16[256,1536]{1,0:T(8,128)(2,1)S(1)}, bf16[256,1536]{1,0:T(8,128)(2,1)S(1)}, u32[]{:S(2)}, u32[]{:S(2)}) collective-permute-start(bf16[256,1536]{1,0:T(8,128)(2,1)S(1)} %pack.1.refs_0_.refs_2_.after_ref.refs_3_), channel_id=1, source_target_pairs={{0,64},{8,24},{16,80},{24,40},{32,96},{40,56},{48,112},{56,8},{64,... | collective-permute-start | bytes 2359304 | tf_op jit(solution)/shard_map/ppermute | solution.py:31
  13.2 1.7 %collective-permute-start.5 = (bf16[256,1536]{1,0:T(8,128)(2,1)S(1)}, bf16[256,1536]{1,0:T(8,128)(2,1)S(1)}, u32[]{:S(2)}, u32[]{:S(2)}) collective-permute-start(bf16[256,1536]{1,0:T(8,128)(2,1)S(1)} %pack.1.refs_0_.refs_2_.after_ref.refs_3_), channel_id=1, source_target_pairs={{0,192},{8,56},{16,208},{24,8},{32,224},{40,24},{48,240},{56,40},{... | collective-permute-start | bytes 2359304 | tf_op jit(solution)/shard_map/ppermute | solution.py:31
  14.9 1.9 %collective-permute-start.4 = (bf16[256,1536]{1,0:T(8,128)(2,1)S(1)}, bf16[256,1536]{1,0:T(8,128)(2,1)S(1)}, u32[]{:S(2)}, u32[]{:S(2)}) collective-permute-start(bf16[256,1536]{1,0:T(8,128)(2,1)S(1)} %pack.1.refs_0_.refs_2_.after_ref.refs_3_), channel_id=1, source_target_pairs={{0,128},{8,40},{16,144},{24,56},{32,160},{40,8},{48,176},{56,24},{... | collective-permute-start | bytes 2359304 | tf_op jit(solution)/shard_map/ppermute | solution.py:31
  16.9 2.0 %collective-permute-start.7 = (bf16[2,2,32,1536]{3,2,1,0:T(8,128)(2,1)S(1)}, bf16[2,2,32,1536]{3,2,1,0:T(8,128)(2,1)S(1)}, u32[]{:S(2)}, u32[]{:S(2)}) collective-permute-start(bf16[2,2,32,1536]{3,2,1,0:T(8,128)(2,1)S(1)} %get-tuple-element.20), channel_id=1, source_target_pairs={{0,1},{1,2},{2,3},{3,4},{4,5},{5,6},{6,7},{7,0},{8,9},{9,10},{10,1... | collective-permute-start | bytes 1179656 | tf_op jit(solution)/shard_map/ppermute | solution.py:20
  18.9 4.0 %collective-permute-start.8 = (bf16[2,2,32,1536]{3,2,1,0:T(8,128)(2,1)S(1)}, bf16[2,2,32,1536]{3,2,1,0:T(8,128)(2,1)S(1)}, u32[]{:S(2)}, u32[]{:S(2)}) collective-permute-start(bf16[2,2,32,1536]{3,2,1,0:T(8,128)(2,1)S(1)} %get-tuple-element.21), channel_id=1, source_target_pairs={{0,7},{1,0},{2,1},{3,2},{4,3},{5,4},{6,5},{7,6},{8,15},{9,8},{10,9... | collective-permute-start | bytes 1179656 | tf_op jit(solution)/shard_map/ppermute | solution.py:20
  22.9 1.5 %near_part.3.refs_3_.base_ref = f32[768,1536]{1,0:T(8,128)S(1)} custom-call(bf16[768,2048]{1,0:T(8,128)(2,1)S(1)} %get-tuple-element.18.act_ref, f32[1536]{0:T(1024)S(1)} %copy-done.6, bf16[256,1536]{1,0:T(8,128)(2,1)S(1)} %pack.1.refs_0_.refs_2_.after_ref.refs_3_, bf16[256,1536]{1,0:T(8,128)(2,1)S(1)} %collective-permute-done.3.refs_1_.refs_2_.refs_7_, ...), custom_call_target="tpu_custom_call" | custom-call | flops 28311552 | bytes 131072 | tf_op jit(solution)/shard_map/near_part/pallas_call | solution.py:204
  24.5 6.1 %collective-permute-done.7.left_ref = bf16[2,2,32,1536]{3,2,1,0:T(8,128)(2,1)S(1)} collective-permute-done((bf16[2,2,32,1536]{3,2,1,0:T(8,128)(2,1)S(1)}, bf16[2,2,32,1536]{3,2,1,0:T(8,128)(2,1)S(1)}, u32[]{:S(2)}, u32[]{:S(2)}) %collective-permute-start.7) | collective-permute-done | bytes 393248 | tf_op jit(solution)/shard_map/ppermute | solution.py:20
  30.6 2.9 %make_target.1 = (f32[768,1536]{1,0:T(8,128)S(1)}, f32[768,128]{1,0:T(8,128)S(1)}) custom-call(s32[2,6]{1,0:T(2,128)S(1)} %copy-done.7, bf16[2,2,32,1536]{3,2,1,0:T(8,128)(2,1)S(1)} %collective-permute-done.7.left_ref, bf16[2,3,32,1536]{3,2,1,0:T(8,128)(2,1)S(1)} %copy-done.2, bf16[2,2,32,1536]{3,2,1,0:T(8,128)(2,1)S(1)} %collective-permute-done.8.right_ref, ...), custom_call_target="tpu_custom_call" | custom-call | flops 8257536 | bytes 147456 | tf_op jit(solution)/shard_map/make_target/pallas_call | solution.py:170
  33.5 0.9 collective-permute-done.4.refs_0_
  35.0 2.2 %near_part.4.base_ref = f32[768,1536]{1,0:T(8,128)S(1)} custom-call(bf16[768,2048]{1,0:T(8,128)(2,1)S(1)} %get-tuple-element.18.act_ref, f32[768,1536]{1,0:T(8,128)S(1)} %near_part.3.refs_3_.base_ref, bf16[256,1536]{1,0:T(8,128)(2,1)S(1)} %get-tuple-element.23.refs_0_.refs_1_, bf16[256,1536]{1,0:T(8,128)(2,1)S(1)} %get-tuple-element.24.refs_1_.refs_2_, ...), custom_call_target="tpu_custom_call" | custom-call | flops 28311552 | bytes 131072 | tf_op jit(solution)/shard_map/near_part/pallas_call | solution.py:204
  37.9 1.5 %near_part.5.near_ref = f32[768,1536]{1,0:T(8,128)S(1)} custom-call(bf16[768,2048]{1,0:T(8,128)(2,1)S(1)} %get-tuple-element.18.act_ref, f32[768,1536]{1,0:T(8,128)S(1)} %near_part.4.base_ref, bf16[256,1536]{1,0:T(8,128)(2,1)S(1)} %collective-permute-done.9.refs_0_.refs_5_, bf16[256,1536]{1,0:T(8,128)(2,1)S(1)} %collective-permute-done.10.refs_1_.refs_6_, ...), custom_call_target="tpu_custom_call" | custom-call | flops 28311552 | bytes 131072 | tf_op jit(solution)/shard_map/near_part/pallas_call | solution.py:204
  39.4 2.8 %out_grads.1.refs_1_.grad_ref = bf16[768,1536]{1,0:T(8,128)(2,1)S(1)} custom-call(s32[2]{0:T(128)S(1)} %copy-done.8, f32[768,1536]{1,0:T(8,128)S(1)} %near_part.5.near_ref, bf16[768,2048]{1,0:T(8,128)(2,1)S(1)} %get-tuple-element.18.act_ref, f32[768,1536]{1,0:T(8,128)S(1)} %get-tuple-element.26.target_ref, ...), custom_call_target="tpu_custom_call" | custom-call | flops 18874368 | bytes 245760 | tf_op jit(solution)/shard_map/out_grads/pallas_call | solution.py:258
  43.2 2.0 %outer.5.refs_0_ = bf16[768,1536]{1,0:T(8,128)(2,1)S(1)} custom-call(bf16[2048,768]{1,0:T(8,128)(2,1)S(1)} %get-tuple-element.19.after_ref.refs_0_, bf16[768,1536]{1,0:T(8,128)(2,1)S(1)} %out_grads.1.refs_1_.grad_ref, bf16[256,1536]{1,0:T(8,128)(2,1)S(1)} %outer.4.refs_2_), custom_call_target="tpu_custom_call" | custom-call | flops 28311552 | bytes 65536 | tf_op jit(solution)/shard_map/outer/pallas_call | solution.py:296
  46.5 2.5 %collective-permute-start.16 = (bf16[256,1536]{1,0:T(8,128)(2,1)S(1)}, bf16[256,1536]{1,0:T(8,128)(2,1)S(1)}, u32[]{:S(2)}, u32[]{:S(2)}) collective-permute-start(bf16[256,1536]{1,0:T(8,128)(2,1)S(1)} %outer.6.refs_3_), channel_id=1, source_target_pairs={{0,128},{8,40},{16,144},{24,56},{32,160},{40,8},{48,176},{56,24},{... | collective-permute-start | bytes 2359304 | tf_op jit(solution)/shard_map/ppermute | solution.py:31
  49.9 2.0 %outer.7 = (bf16[256,1536]{1,0:T(8,128)(2,1)S(1)}, bf16[256,1536]{1,0:T(8,128)(2,1)S(1)}, f32[256,1536]{1,0:T(8,128)S(1)}) custom-call(bf16[2048,768]{1,0:T(8,128)(2,1)S(1)} %get-tuple-element.19.after_ref.refs_0_, bf16[768,1536]{1,0:T(8,128)(2,1)S(1)} %out_grads.1.refs_1_.grad_ref, bf16[768,1536]{1,0:T(8,128)(2,1)S(1)} %collective-permute-done.13.refs_2_, ...), custom_call_target="tpu_custom_call" | custom-call | flops 28311552 | bytes 65536 | tf_op jit(solution)/shard_map/outer/pallas_call | solution.py:296
  51.9 1.5 %collective-permute-start.14 = (bf16[256,1536]{1,0:T(8,128)(2,1)S(1)}, bf16[256,1536]{1,0:T(8,128)(2,1)S(1)}, u32[]{:S(2)}, u32[]{:S(2)}) collective-permute-start(bf16[256,1536]{1,0:T(8,128)(2,1)S(1)} %get-tuple-element.27.refs_8_), channel_id=1, source_target_pairs={{0,64},{8,24},{16,80},{24,40},{32,96},{40,56},{48,112},{56,8},{64,... | collective-permute-start | bytes 2359304 | tf_op jit(solution)/shard_map/ppermute | solution.py:31
  53.4 1.8 %collective-permute-start.15 = (bf16[256,1536]{1,0:T(8,128)(2,1)S(1)}, bf16[256,1536]{1,0:T(8,128)(2,1)S(1)}, u32[]{:S(2)}, u32[]{:S(2)}) collective-permute-start(bf16[256,1536]{1,0:T(8,128)(2,1)S(1)} %get-tuple-element.29.refs_0_), channel_id=1, source_target_pairs={{0,192},{8,56},{16,208},{24,8},{32,224},{40,24},{48,240},{56,40},{... | collective-permute-start | bytes 2359304 | tf_op jit(solution)/shard_map/ppermute | solution.py:31
  55.2 1.0 whole_weight.1.w_ref
  56.3 6.1 %pre_grads.2 = (bf16[768,2048]{1,0:T(8,128)(2,1)}, f32[8,128]{1,0:T(8,128)S(1)}) custom-call(bf16[768,1536]{1,0:T(8,128)(2,1)S(1)} %out_grads.1.refs_1_.grad_ref, bf16[2048,1536]{1,0:T(8,128)(2,1)S(1)} %whole_weight.1.w_ref, bf16[768,2048]{1,0:T(8,128)(2,1)S(1)} %bitcast.8, bf16[256,1536]{1,0:T(8,128)(2,1)S(1)} %get-tuple-element.29.refs_0_), custom_call_target="tpu_custom_call" | custom-call | flops 56623104 | bytes 196608 | tf_op jit(solution)/shard_map/pre_grads/pallas_call | solution.py:363
  62.4 6.1 %collective-permute-done.14 = bf16[256,1536]{1,0:T(8,128)(2,1)S(1)} collective-permute-done((bf16[256,1536]{1,0:T(8,128)(2,1)S(1)}, bf16[256,1536]{1,0:T(8,128)(2,1)S(1)}, u32[]{:S(2)}, u32[]{:S(2)}) %collective-permute-start.14) | collective-permute-done | bytes 786464 | tf_op jit(solution)/shard_map/ppermute | solution.py:31
  69.1 1.9 %collective-permute-start.17 = (bf16[64,1536]{1,0:T(8,128)(2,1)S(1)}, bf16[64,1536]{1,0:T(8,128)(2,1)S(1)}, u32[]{:S(2)}, u32[]{:S(2)}) collective-permute-start(bf16[64,1536]{1,0:T(8,128)(2,1)S(1)} %get-tuple-element.36), channel_id=1, source_target_pairs={{0,16},{8,72},{16,32},{24,88},{32,48},{40,104},{48,0},{56,120},{64... | collective-permute-start | bytes 589832 | tf_op jit(solution)/shard_map/ppermute | solution.py:31
  71.0 1.3 %collective-permute-start.19 = (bf16[64,1536]{1,0:T(8,128)(2,1)S(1)}, bf16[64,1536]{1,0:T(8,128)(2,1)S(1)}, u32[]{:S(2)}, u32[]{:S(2)}) collective-permute-start(bf16[64,1536]{1,0:T(8,128)(2,1)S(1)} %get-tuple-element.37), channel_id=1, source_target_pairs={{0,32},{8,136},{16,48},{24,152},{32,0},{40,168},{48,16},{56,184},{... | collective-permute-start | bytes 589832 | tf_op jit(solution)/shard_map/ppermute | solution.py:31
  72.7 2.5 %pre_grads.3 = (bf16[768,2048]{1,0:T(8,128)(2,1)}, f32[8,128]{1,0:T(8,128)S(1)}) custom-call(bf16[768,1536]{1,0:T(8,128)(2,1)S(1)} %out_grads.1.refs_1_.grad_ref, bf16[2048,1536]{1,0:T(8,128)(2,1)S(1)} %whole_weight.1.w_ref, bf16[768,2048]{1,0:T(8,128)(2,1)S(1)} %bitcast.9, ...), custom_call_target="tpu_custom_call", output_to_operand_aliasing={{0}: (4, {})} | custom-call | flops 18874368 | bytes 65536 | tf_op jit(solution)/shard_map/pre_grads/pallas_call | solution.py:363
  75.2 1.1 collective-permute-done.17
  76.3 1.9 %collective-permute-done.19 = bf16[64,1536]{1,0:T(8,128)(2,1)S(1)} collective-permute-done((bf16[64,1536]{1,0:T(8,128)(2,1)S(1)}, bf16[64,1536]{1,0:T(8,128)(2,1)S(1)}, u32[]{:S(2)}, u32[]{:S(2)}) %collective-permute-start.19) | collective-permute-done | bytes 196640 | tf_op jit(solution)/shard_map/ppermute | solution.py:31
  78.2 2.0 %collective-permute-done.18 = bf16[64,1536]{1,0:T(8,128)(2,1)S(1)} collective-permute-done((bf16[64,1536]{1,0:T(8,128)(2,1)S(1)}, bf16[64,1536]{1,0:T(8,128)(2,1)S(1)}, u32[]{:S(2)}, u32[]{:S(2)}) %collective-permute-start.18) | collective-permute-done | bytes 196640 | tf_op jit(solution)/shard_map/ppermute | solution.py:31
  80.3 18.0 %all_to_all.15 = bf16[8,8,1536]{2,1,0:T(8,128)(2,1)S(1)} all-to-all(bf16[8,8,1536]{2,1,0:T(8,128)(2,1)S(1)} %fusion), channel_id=1, replica_groups=mesh['y'=4,'x'=4,'c'=2,'z'=8] {'z'}, dimensions={0} | all-to-all | bytes 393216 | tf_op jit(solution)/shard_map/all_to_all | solution.py:425
  98.4 12.2 %all_to_all.16 = bf16[8,8,1536]{2,1,0:T(8,128)(2,1)S(1)} all-to-all(bf16[8,8,1536]{2,1,0:T(8,128)(2,1)S(1)} %broadcast_in_dim.2), channel_id=1, replica_groups=mesh['y'=4,'x'=4,'c'=2,'z'=8] {'z'}, dimensions={0} | all-to-all | bytes 393216 | tf_op jit(solution)/shard_map/all_to_all | solution.py:428
  (55 shorter events, 7.9 us)
Async XLA Ops:
  0.6 9.6 %collective-permute-start.1 = (bf16[64,1536]{1,0:T(8,128)(2,1)}, bf16[64,1536]{1,0:T(8,128)(2,1)S(1)}, u32[]{:S(2)}, u32[]{:S(2)}) collective-permute-start(bf16[64,1536]{1,0:T(8,128)(2,1)} %own_ref.1), channel_id=1, source_target_pairs={{0,48},{8,200},{16,0},{24,216},{32,16},{40,232},{48,32},{56,248},{... | collective-permute-start | bytes 589832 | tf_op jit(solution)/shard_map/ppermute | solution.py:31
  1.5 8.7 %collective-permute-start = (bf16[64,1536]{1,0:T(8,128)(2,1)}, bf16[64,1536]{1,0:T(8,128)(2,1)S(1)}, u32[]{:S(2)}, u32[]{:S(2)}) collective-permute-start(bf16[64,1536]{1,0:T(8,128)(2,1)} %own_ref.1), channel_id=1, source_target_pairs={{0,16},{8,72},{16,32},{24,88},{32,48},{40,104},{48,0},{56,120},{64... | collective-permute-start | bytes 589832 | tf_op jit(solution)/shard_map/ppermute | solution.py:31
  3.9 7.4 %collective-permute-start.2 = (bf16[64,1536]{1,0:T(8,128)(2,1)}, bf16[64,1536]{1,0:T(8,128)(2,1)S(1)}, u32[]{:S(2)}, u32[]{:S(2)}) collective-permute-start(bf16[64,1536]{1,0:T(8,128)(2,1)} %own_ref.1), channel_id=1, source_target_pairs={{0,32},{8,136},{16,48},{24,152},{32,0},{40,168},{48,16},{56,184},{... | collective-permute-start | bytes 589832 | tf_op jit(solution)/shard_map/ppermute | solution.py:31
  4.4 1.9 %copy-start = (bf16[2,6,64,2048]{3,2,1,0:T(8,128)(2,1)S(1)}, bf16[2,6,64,2048]{3,2,1,0:T(8,128)(2,1)}, u32[]{:S(2)}) copy-start(bf16[2,6,64,2048]{3,2,1,0:T(8,128)(2,1)} %param.13) | copy-start | bytes 9437188
  6.3 5.1 %copy-start.3 = (bf16[64,1536]{1,0:T(8,128)(2,1)S(1)}, bf16[64,1536]{1,0:T(8,128)(2,1)}, u32[]{:S(2)}) copy-start(bf16[64,1536]{1,0:T(8,128)(2,1)} %own_ref.1) | copy-start | bytes 589828
  11.3 5.5 %copy-start.2 = (bf16[2,3,32,1536]{3,2,1,0:T(8,128)(2,1)S(1)}, bf16[2,3,32,1536]{3,2,1,0:T(8,128)(2,1)}, u32[]{:S(2)}) copy-start(bf16[2,3,32,1536]{3,2,1,0:T(8,128)(2,1)} %mid_ref.1) | copy-start | bytes 1769476
  11.4 11.5 %copy-start.6 = (f32[1536]{0:T(1024)S(1)}, f32[1536]{0:T(1024)}, u32[]{:S(2)}) copy-start(f32[1536]{0:T(1024)} %base_ref.1) | copy-start | bytes 18436
  11.4 5.5 %collective-permute-start.3 = (bf16[256,1536]{1,0:T(8,128)(2,1)S(1)}, bf16[256,1536]{1,0:T(8,128)(2,1)S(1)}, u32[]{:S(2)}, u32[]{:S(2)}) collective-permute-start(bf16[256,1536]{1,0:T(8,128)(2,1)S(1)} %pack.1.refs_0_.refs_2_.after_ref.refs_3_), channel_id=1, source_target_pairs={{0,8},{8,0},{1,9},{9,1},{2,10},{10,2},{3,11},{11,3},{4,12},{12,4},... | collective-permute-start | bytes 2359304 | tf_op jit(solution)/shard_map/ppermute | solution.py:20
  11.6 21.9 %collective-permute-start.6 = (bf16[256,1536]{1,0:T(8,128)(2,1)S(1)}, bf16[256,1536]{1,0:T(8,128)(2,1)S(1)}, u32[]{:S(2)}, u32[]{:S(2)}) collective-permute-start(bf16[256,1536]{1,0:T(8,128)(2,1)S(1)} %pack.1.refs_0_.refs_2_.after_ref.refs_3_), channel_id=1, source_target_pairs={{0,64},{8,24},{16,80},{24,40},{32,96},{40,56},{48,112},{56,8},{64,... | collective-permute-start | bytes 2359304 | tf_op jit(solution)/shard_map/ppermute | solution.py:31
  13.2 20.3 %collective-permute-start.5 = (bf16[256,1536]{1,0:T(8,128)(2,1)S(1)}, bf16[256,1536]{1,0:T(8,128)(2,1)S(1)}, u32[]{:S(2)}, u32[]{:S(2)}) collective-permute-start(bf16[256,1536]{1,0:T(8,128)(2,1)S(1)} %pack.1.refs_0_.refs_2_.after_ref.refs_3_), channel_id=1, source_target_pairs={{0,192},{8,56},{16,208},{24,8},{32,224},{40,24},{48,240},{56,40},{... | collective-permute-start | bytes 2359304 | tf_op jit(solution)/shard_map/ppermute | solution.py:31
  14.9 19.6 %collective-permute-start.4 = (bf16[256,1536]{1,0:T(8,128)(2,1)S(1)}, bf16[256,1536]{1,0:T(8,128)(2,1)S(1)}, u32[]{:S(2)}, u32[]{:S(2)}) collective-permute-start(bf16[256,1536]{1,0:T(8,128)(2,1)S(1)} %pack.1.refs_0_.refs_2_.after_ref.refs_3_), channel_id=1, source_target_pairs={{0,128},{8,40},{16,144},{24,56},{32,160},{40,8},{48,176},{56,24},{... | collective-permute-start | bytes 2359304 | tf_op jit(solution)/shard_map/ppermute | solution.py:31
  16.9 13.7 %collective-permute-start.7 = (bf16[2,2,32,1536]{3,2,1,0:T(8,128)(2,1)S(1)}, bf16[2,2,32,1536]{3,2,1,0:T(8,128)(2,1)S(1)}, u32[]{:S(2)}, u32[]{:S(2)}) collective-permute-start(bf16[2,2,32,1536]{3,2,1,0:T(8,128)(2,1)S(1)} %get-tuple-element.20), channel_id=1, source_target_pairs={{0,1},{1,2},{2,3},{3,4},{4,5},{5,6},{6,7},{7,0},{8,9},{9,10},{10,1... | collective-permute-start | bytes 1179656 | tf_op jit(solution)/shard_map/ppermute | solution.py:20
  18.9 11.7 %collective-permute-start.8 = (bf16[2,2,32,1536]{3,2,1,0:T(8,128)(2,1)S(1)}, bf16[2,2,32,1536]{3,2,1,0:T(8,128)(2,1)S(1)}, u32[]{:S(2)}, u32[]{:S(2)}) collective-permute-start(bf16[2,2,32,1536]{3,2,1,0:T(8,128)(2,1)S(1)} %get-tuple-element.21), channel_id=1, source_target_pairs={{0,7},{1,0},{2,1},{3,2},{4,3},{5,4},{6,5},{7,6},{8,15},{9,8},{10,9... | collective-permute-start | bytes 1179656 | tf_op jit(solution)/shard_map/ppermute | solution.py:20
  22.9 7.6 %copy-start.4 = (f32[1536]{0:T(1024)S(1)}, f32[1536]{0:T(1024)}, u32[]{:S(2)}) copy-start(f32[1536]{0:T(1024)} %gain_ref.1) | copy-start | bytes 18436
  22.9 7.6 %copy-start.5 = (f32[1536]{0:T(1024)S(1)}, f32[1536]{0:T(1024)}, u32[]{:S(2)}) copy-start(f32[1536]{0:T(1024)} %bias_ref.1) | copy-start | bytes 18436
  22.9 7.6 %copy-start.7 = (s32[2,6]{1,0:T(2,128)S(1)}, s32[2,6]{1,0:T(2,128)}, u32[]{:S(2)}) copy-start(s32[2,6]{1,0:T(2,128)} %source_ref.1) | copy-start | bytes 148
  34.4 2.7 %collective-permute-start.9 = (bf16[256,1536]{1,0:T(8,128)(2,1)S(1)}, bf16[256,1536]{1,0:T(8,128)(2,1)S(1)}, u32[]{:S(2)}, u32[]{:S(2)}) collective-permute-start(bf16[256,1536]{1,0:T(8,128)(2,1)S(1)} %get-tuple-element.23.refs_0_.refs_1_), channel_id=1, source_target_pairs={{0,8},{8,0},{1,9},{9,1},{2,10},{10,2},{3,11},{11,3},{4,12},{12,4},... | collective-permute-start | bytes 2359304 | tf_op jit(solution)/shard_map/ppermute | solution.py:20
  34.5 3.4 %collective-permute-start.10 = (bf16[256,1536]{1,0:T(8,128)(2,1)S(1)}, bf16[256,1536]{1,0:T(8,128)(2,1)S(1)}, u32[]{:S(2)}, u32[]{:S(2)}) collective-permute-start(bf16[256,1536]{1,0:T(8,128)(2,1)S(1)} %get-tuple-element.24.refs_1_.refs_2_), channel_id=1, source_target_pairs={{0,8},{8,0},{1,9},{9,1},{2,10},{10,2},{3,11},{11,3},{4,12},{12,4},... | collective-permute-start | bytes 2359304 | tf_op jit(solution)/shard_map/ppermute | solution.py:20
  35.0 4.5 %collective-permute-start.11 = (bf16[256,1536]{1,0:T(8,128)(2,1)S(1)}, bf16[256,1536]{1,0:T(8,128)(2,1)S(1)}, u32[]{:S(2)}, u32[]{:S(2)}) collective-permute-start(bf16[256,1536]{1,0:T(8,128)(2,1)S(1)} %get-tuple-element.25.refs_2_.refs_0_), channel_id=1, source_target_pairs={{0,8},{8,0},{1,9},{9,1},{2,10},{10,2},{3,11},{11,3},{4,12},{12,4},... | collective-permute-start | bytes 2359304 | tf_op jit(solution)/shard_map/ppermute | solution.py:20
  37.2 2.2 %copy-start.8 = (s32[2]{0:T(128)S(1)}, s32[2]{0:T(128)}, u32[]{:S(2)}) copy-start(s32[2]{0:T(128)} %time_ref.1) | copy-start | bytes 28
  43.0 2.4 %collective-permute-start.12 = (bf16[256,1536]{1,0:T(8,128)(2,1)S(1)}, bf16[256,1536]{1,0:T(8,128)(2,1)S(1)}, u32[]{:S(2)}, u32[]{:S(2)}) collective-permute-start(bf16[256,1536]{1,0:T(8,128)(2,1)S(1)} %outer.4.refs_2_), channel_id=1, source_target_pairs={{0,8},{8,0},{1,9},{9,1},{2,10},{10,2},{3,11},{11,3},{4,12},{12,4},... | collective-permute-start | bytes 2359304 | tf_op jit(solution)/shard_map/ppermute | solution.py:20
  45.4 4.5 %collective-permute-start.13 = (bf16[768,1536]{1,0:T(8,128)(2,1)S(1)}, bf16[768,1536]{1,0:T(8,128)(2,1)S(1)}, u32[]{:S(2)}, u32[]{:S(2)}) collective-permute-start(bf16[768,1536]{1,0:T(8,128)(2,1)S(1)} %gate.7.refs_3_), channel_id=1, source_target_pairs={{0,8},{8,0},{1,9},{9,1},{2,10},{10,2},{3,11},{11,3},{4,12},{12,4},... | collective-permute-start | bytes 7077896 | tf_op jit(solution)/shard_map/ppermute | solution.py:20
  46.5 15.9 %collective-permute-start.16 = (bf16[256,1536]{1,0:T(8,128)(2,1)S(1)}, bf16[256,1536]{1,0:T(8,128)(2,1)S(1)}, u32[]{:S(2)}, u32[]{:S(2)}) collective-permute-start(bf16[256,1536]{1,0:T(8,128)(2,1)S(1)} %outer.6.refs_3_), channel_id=1, source_target_pairs={{0,128},{8,40},{16,144},{24,56},{32,160},{40,8},{48,176},{56,24},{... | collective-permute-start | bytes 2359304 | tf_op jit(solution)/shard_map/ppermute | solution.py:31
  51.9 16.6 %collective-permute-start.14 = (bf16[256,1536]{1,0:T(8,128)(2,1)S(1)}, bf16[256,1536]{1,0:T(8,128)(2,1)S(1)}, u32[]{:S(2)}, u32[]{:S(2)}) collective-permute-start(bf16[256,1536]{1,0:T(8,128)(2,1)S(1)} %get-tuple-element.27.refs_8_), channel_id=1, source_target_pairs={{0,64},{8,24},{16,80},{24,40},{32,96},{40,56},{48,112},{56,8},{64,... | collective-permute-start | bytes 2359304 | tf_op jit(solution)/shard_map/ppermute | solution.py:31
  53.4 2.9 %copy-start.1 = (bf16[2,6,64,2048]{3,2,1,0:T(8,128)(2,1)S(1)}, bf16[2,6,64,2048]{3,2,1,0:T(8,128)(2,1)}, u32[]{:S(2)}) copy-start(bf16[2,6,64,2048]{3,2,1,0:T(8,128)(2,1)} %param.13) | copy-start | bytes 9437188
  53.4 15.1 %collective-permute-start.15 = (bf16[256,1536]{1,0:T(8,128)(2,1)S(1)}, bf16[256,1536]{1,0:T(8,128)(2,1)S(1)}, u32[]{:S(2)}, u32[]{:S(2)}) collective-permute-start(bf16[256,1536]{1,0:T(8,128)(2,1)S(1)} %get-tuple-element.29.refs_0_), channel_id=1, source_target_pairs={{0,192},{8,56},{16,208},{24,8},{32,224},{40,24},{48,240},{56,40},{... | collective-permute-start | bytes 2359304 | tf_op jit(solution)/shard_map/ppermute | solution.py:31
  69.1 7.2 %collective-permute-start.17 = (bf16[64,1536]{1,0:T(8,128)(2,1)S(1)}, bf16[64,1536]{1,0:T(8,128)(2,1)S(1)}, u32[]{:S(2)}, u32[]{:S(2)}) collective-permute-start(bf16[64,1536]{1,0:T(8,128)(2,1)S(1)} %get-tuple-element.36), channel_id=1, source_target_pairs={{0,16},{8,72},{16,32},{24,88},{32,48},{40,104},{48,0},{56,120},{64... | collective-permute-start | bytes 589832 | tf_op jit(solution)/shard_map/ppermute | solution.py:31
  71.0 7.3 %collective-permute-start.19 = (bf16[64,1536]{1,0:T(8,128)(2,1)S(1)}, bf16[64,1536]{1,0:T(8,128)(2,1)S(1)}, u32[]{:S(2)}, u32[]{:S(2)}) collective-permute-start(bf16[64,1536]{1,0:T(8,128)(2,1)S(1)} %get-tuple-element.37), channel_id=1, source_target_pairs={{0,32},{8,136},{16,48},{24,152},{32,0},{40,168},{48,16},{56,184},{... | collective-permute-start | bytes 589832 | tf_op jit(solution)/shard_map/ppermute | solution.py:31
  72.2 8.0 %collective-permute-start.18 = (bf16[64,1536]{1,0:T(8,128)(2,1)S(1)}, bf16[64,1536]{1,0:T(8,128)(2,1)S(1)}, u32[]{:S(2)}, u32[]{:S(2)}) collective-permute-start(bf16[64,1536]{1,0:T(8,128)(2,1)S(1)} %get-tuple-element.38), channel_id=1, source_target_pairs={{0,48},{8,200},{16,0},{24,216},{32,16},{40,232},{48,32},{56,248},{... | collective-permute-start | bytes 589832 | tf_op jit(solution)/shard_map/ppermute | solution.py:31

commit v3 on v2

--- a/solution.py
+++ b/solution.py
@@ -214,7 +214,7 @@
 
 
 def grad_kernel(time_ref, near_ref, act_ref, target_ref, tsum_ref, *refs):
-    pieces, (out_ref, proj_ref, w_ref, sem_ref) = refs[:1], refs[1:]
+    pieces, (rows_ref, out_ref, away_ref, own_ref, proj_ref, sum_ref, w_ref, sem_ref) = refs[:1], refs[1:]
     copies = [
         pltpu.make_async_copy(piece_ref, w_ref.at[k * 256 : k * 256 + 256], sem_ref.at[k])
         for k, piece_ref in enumerate(pieces)
@@ -249,26 +249,36 @@
             near = scaled * inv
             along = scaled * (cross_sum * inv) / pn2
             out_ref[rows, :] = (near * target_ref[rows, :] - along * proj_ref[rows, :]).astype(bf16)
-
-
-def out_grads(timesteps, near, active, target, tsum, pieces):
+        far_rows = jnp.concatenate([rows_ref[1024:1280, here_rows], rows_ref[0:256, here_rows]], axis=0)
+        term = jnp.dot(far_rows, out_ref[here_rows, :], preferred_element_type=f32)
+        sum_ref[...] = term if first == 0 else sum_ref[...] + term
+    away_ref[...] = sum_ref[0:256, :].astype(bf16)
+    own_ref[...] = sum_ref[256:512, :]
+
+
+def out_grads(timesteps, near, active, target, tsum, pieces, rows):
     tokens, width = target.shape
     whole = pl.BlockSpec(memory_space=VMEM)
     smem = pl.BlockSpec(memory_space=SMEM)
     return pl.pallas_call(
         grad_kernel,
-        in_specs=[smem] + [whole] * 4 + [pl.BlockSpec(memory_space=pl.ANY)] * len(pieces),
-        out_specs=whole,
-        out_shape=jax.ShapeDtypeStruct((tokens, width), bf16),
+        in_specs=[smem] + [whole] * 4 + [pl.BlockSpec(memory_space=pl.ANY)] * len(pieces) + [whole],
+        out_specs=[whole] * 3,
+        out_shape=[
+            jax.ShapeDtypeStruct((tokens, width), bf16),
+            jax.ShapeDtypeStruct((256, width), bf16),
+            jax.ShapeDtypeStruct((256, width), f32),
+        ],
         scratch_shapes=[
             pltpu.VMEM((tokens, width), f32),
+            pltpu.VMEM((512, width), f32),
             pltpu.VMEM((256, width), bf16),
             pltpu.SemaphoreType.DMA((1,)),
         ],
-        compiler_params=params(20),
+        compiler_params=params(24),
         cost_estimate=cost(2 * tokens * 512 * width, 15 * MIB),
         name="out_grads",
-    )(timesteps, near, active, target, tsum, *pieces)
+    )(timesteps, near, active, target, tsum, *pieces, rows)
 
 
 def outer_kernel(first, blocks, outs, added, *refs):
@@ -404,14 +414,13 @@
     other = [shift(piece, "c", 1) for piece in mine]
     close = near_part(active, close, mine[1:] + mine[:1], 512, line)
     close = near_part(active, close, other[1:], 1280, line)
-    grad = out_grads(timesteps, close, active, target, tsum, other[:1])
+    grad, away_far, far = out_grads(timesteps, close, active, target, tsum, other[:1], rows)
     mine, other = mine + [line], other + [other_line]
-    (away_far,) = outer(rows, grad, 1024, 256, ((0, 256, bf16),))
     back_far = shift(away_far, "c", 1)
     (away,) = outer(rows, grad, 1280, 768, ((0, 768, bf16),), after=away_far)
     (away,) = gate((away,), (back_far,))
     back = shift(away, "c", 1)
-    (far,) = outer(rows, grad, 0, 256, ((0, 256, bf16),), back_far, after=away)
+    far = (far + back_far.astype(f32)).astype(bf16)
     kept_outs = ((0, 256, bf16), (256, 256, bf16), (512, 256, f32))
     to_one, to_three, own = outer(rows, grad, 256, 768, kept_outs, back, after=far)
     weight = whole_weight(mine + other, to_one)

time: 112 us -> 112 us (level)
    pallas_call x1, Pallas kernels: 2.8 us -> 4.39 us  [out_grads(): pl.pallas_call(grad_kernel, in_specs=[smem] + [whole] * 4 + [pl.BlockSpec...]
    pallas_call x4 -> x2, Pallas kernels: 5.53 us -> 3.97 us  [outer(): pl.pallas_call(functools.partial(outer_kernel, start, count // 256, outs,...]
  transfers between devices with their start and end apart: 20 -> 20, of which waited for: 10 -> 10; matrix products, arithmetic and copies ran while one was open for 0% -> 0% of each run, Pallas kernels for 24% -> 23%
where the time goes in v3:
time: 112 us
  Pallas kernels  30.2 us (27%)
  blocking collectives  30.2 us (27%)
  starting transfers between devices  25.6 us (23%)
  waiting for transfers between devices  21 us (19%)
  local copies, waits for them, and re-layouts  2.06 us (2%)
  other arithmetic  1.63 us (1%)
    ppermute x12, starting transfers between devices, turn(): return lax.ppermute(block, ('y', 'x', 'c'), pairs)  18.3 us
    all_to_all x1, blocking collectives, body(): parts = lax.all_to_all(block, 'z', 0, 0, tiled=True)  18 us
    ppermute x12, waiting for transfers between devices, turn(): return lax.ppermute(block, ('y', 'x', 'c'), pairs)  12.6 us
    all_to_all x1, blocking collectives, body(): weight_grad = lax.all_to_all(total, 'z', 0, 0, tiled=True).astype(f32)  12.2 us
    pallas_call x2, Pallas kernels, pre_grads(): pl.pallas_call(pre_kernel, grid=(count,), in_specs=[pl.BlockSpec((tokens,...  8.64 us
    ppermute x8, waiting for transfers between devices, shift(): lax.ppermute(block, axis, [(i, (i + step) % count) for i in range(count)])  8.36 us
    ppermute x8, starting transfers between devices, shift(): lax.ppermute(block, axis, [(i, (i + step) % count) for i in range(count)])  7.3 us
    pallas_call x3, Pallas kernels, near_part(): pl.pallas_call(functools.partial(near_kernel, first, base.ndim == 2), in_...  5.29 us
  transfers between devices with their start and end apart: 20, of which 10 were waited for; matrix products, arithmetic and copies ran while one was open for 0% of the time, Pallas kernels for 23%

profile of v3, /device:TPU:6, one launch (start us, length us, event | category | flops | bytes accessed | tf_op | source)
XLA Modules:
  0.0 111.6 jit_solution(3391669158000369381)
XLA Ops:
  1.5 2.4 %collective-permute-start = (bf16[64,1536]{1,0:T(8,128)(2,1)}, bf16[64,1536]{1,0:T(8,128)(2,1)S(1)}, u32[]{:S(2)}, u32[]{:S(2)}) collective-permute-start(bf16[64,1536]{1,0:T(8,128)(2,1)} %own_ref.1), channel_id=1, source_target_pairs={{0,16},{8,72},{16,32},{24,88},{32,48},{40,104},{48,0},{56,120},{64... | collective-permute-start | bytes 589832 | tf_op jit(solution)/shard_map/ppermute | solution.py:31
  4.4 1.9 %copy-done = bf16[2,6,64,2048]{3,2,1,0:T(8,128)(2,1)S(1)} copy-done((bf16[2,6,64,2048]{3,2,1,0:T(8,128)(2,1)S(1)}, bf16[2,6,64,2048]{3,2,1,0:T(8,128)(2,1)}, u32[]{:S(2)}) %copy-start) | copy-done | bytes 3145752
  6.3 4.0 %hidden_rows.1 = (bf16[2048,768]{1,0:T(8,128)(2,1)S(1)}, bf16[768,2048]{1,0:T(8,128)(2,1)S(1)}) custom-call(bf16[768,2048]{1,0:T(8,128)(2,1)S(1)} %bitcast.7), custom_call_target="tpu_custom_call" | custom-call | flops 196608 | bytes 147456 | tf_op jit(solution)/shard_map/hidden_rows/pallas_call | solution.py:118
  10.3 1.1 collective-permute-done.2.far_ref
  11.6 1.5 %collective-permute-start.6 = (bf16[256,1536]{1,0:T(8,128)(2,1)S(1)}, bf16[256,1536]{1,0:T(8,128)(2,1)S(1)}, u32[]{:S(2)}, u32[]{:S(2)}) collective-permute-start(bf16[256,1536]{1,0:T(8,128)(2,1)S(1)} %pack.1.refs_0_.refs_2_.after_ref.refs_3_), channel_id=1, source_target_pairs={{0,64},{8,24},{16,80},{24,40},{32,96},{40,56},{48,112},{56,8},{64,... | collective-permute-start | bytes 2359304 | tf_op jit(solution)/shard_map/ppermute | solution.py:31
  13.2 1.7 %collective-permute-start.5 = (bf16[256,1536]{1,0:T(8,128)(2,1)S(1)}, bf16[256,1536]{1,0:T(8,128)(2,1)S(1)}, u32[]{:S(2)}, u32[]{:S(2)}) collective-permute-start(bf16[256,1536]{1,0:T(8,128)(2,1)S(1)} %pack.1.refs_0_.refs_2_.after_ref.refs_3_), channel_id=1, source_target_pairs={{0,192},{8,56},{16,208},{24,8},{32,224},{40,24},{48,240},{56,40},{... | collective-permute-start | bytes 2359304 | tf_op jit(solution)/shard_map/ppermute | solution.py:31
  14.9 1.9 %collective-permute-start.4 = (bf16[256,1536]{1,0:T(8,128)(2,1)S(1)}, bf16[256,1536]{1,0:T(8,128)(2,1)S(1)}, u32[]{:S(2)}, u32[]{:S(2)}) collective-permute-start(bf16[256,1536]{1,0:T(8,128)(2,1)S(1)} %pack.1.refs_0_.refs_2_.after_ref.refs_3_), channel_id=1, source_target_pairs={{0,128},{8,40},{16,144},{24,56},{32,160},{40,8},{48,176},{56,24},{... | collective-permute-start | bytes 2359304 | tf_op jit(solution)/shard_map/ppermute | solution.py:31
  16.9 2.0 %collective-permute-start.7 = (bf16[2,2,32,1536]{3,2,1,0:T(8,128)(2,1)S(1)}, bf16[2,2,32,1536]{3,2,1,0:T(8,128)(2,1)S(1)}, u32[]{:S(2)}, u32[]{:S(2)}) collective-permute-start(bf16[2,2,32,1536]{3,2,1,0:T(8,128)(2,1)S(1)} %get-tuple-element.23), channel_id=1, source_target_pairs={{0,1},{1,2},{2,3},{3,4},{4,5},{5,6},{6,7},{7,0},{8,9},{9,10},{10,1... | collective-permute-start | bytes 1179656 | tf_op jit(solution)/shard_map/ppermute | solution.py:20
  18.9 4.0 %collective-permute-start.8 = (bf16[2,2,32,1536]{3,2,1,0:T(8,128)(2,1)S(1)}, bf16[2,2,32,1536]{3,2,1,0:T(8,128)(2,1)S(1)}, u32[]{:S(2)}, u32[]{:S(2)}) collective-permute-start(bf16[2,2,32,1536]{3,2,1,0:T(8,128)(2,1)S(1)} %get-tuple-element.24), channel_id=1, source_target_pairs={{0,7},{1,0},{2,1},{3,2},{4,3},{5,4},{6,5},{7,6},{8,15},{9,8},{10,9... | collective-permute-start | bytes 1179656 | tf_op jit(solution)/shard_map/ppermute | solution.py:20
  22.9 1.5 %near_part.3.refs_3_.base_ref = f32[768,1536]{1,0:T(8,128)S(1)} custom-call(bf16[768,2048]{1,0:T(8,128)(2,1)S(1)} %get-tuple-element.21.act_ref, f32[1536]{0:T(1024)S(1)} %copy-done.6, bf16[256,1536]{1,0:T(8,128)(2,1)S(1)} %pack.1.refs_0_.refs_2_.after_ref.refs_3_, bf16[256,1536]{1,0:T(8,128)(2,1)S(1)} %collective-permute-done.3.refs_1_.refs_2_.refs_7_, ...), custom_call_target="tpu_custom_call" | custom-call | flops 28311552 | bytes 131072 | tf_op jit(solution)/shard_map/near_part/pallas_call | solution.py:204
  24.5 6.1 %collective-permute-done.7.left_ref = bf16[2,2,32,1536]{3,2,1,0:T(8,128)(2,1)S(1)} collective-permute-done((bf16[2,2,32,1536]{3,2,1,0:T(8,128)(2,1)S(1)}, bf16[2,2,32,1536]{3,2,1,0:T(8,128)(2,1)S(1)}, u32[]{:S(2)}, u32[]{:S(2)}) %collective-permute-start.7) | collective-permute-done | bytes 393248 | tf_op jit(solution)/shard_map/ppermute | solution.py:20
  30.6 2.9 %make_target.1 = (f32[768,1536]{1,0:T(8,128)S(1)}, f32[768,128]{1,0:T(8,128)S(1)}) custom-call(s32[2,6]{1,0:T(2,128)S(1)} %copy-done.7, bf16[2,2,32,1536]{3,2,1,0:T(8,128)(2,1)S(1)} %collective-permute-done.7.left_ref, bf16[2,3,32,1536]{3,2,1,0:T(8,128)(2,1)S(1)} %copy-done.2, bf16[2,2,32,1536]{3,2,1,0:T(8,128)(2,1)S(1)} %collective-permute-done.8.right_ref, ...), custom_call_target="tpu_custom_call" | custom-call | flops 8257536 | bytes 147456 | tf_op jit(solution)/shard_map/make_target/pallas_call | solution.py:170
  35.0 2.2 %near_part.4.base_ref = f32[768,1536]{1,0:T(8,128)S(1)} custom-call(bf16[768,2048]{1,0:T(8,128)(2,1)S(1)} %get-tuple-element.21.act_ref, f32[768,1536]{1,0:T(8,128)S(1)} %near_part.3.refs_3_.base_ref, bf16[256,1536]{1,0:T(8,128)(2,1)S(1)} %get-tuple-element.26.refs_0_.refs_1_, bf16[256,1536]{1,0:T(8,128)(2,1)S(1)} %get-tuple-element.27.refs_1_.refs_2_, ...), custom_call_target="tpu_custom_call" | custom-call | flops 28311552 | bytes 131072 | tf_op jit(solution)/shard_map/near_part/pallas_call | solution.py:204
  37.9 1.5 %near_part.5.near_ref = f32[768,1536]{1,0:T(8,128)S(1)} custom-call(bf16[768,2048]{1,0:T(8,128)(2,1)S(1)} %get-tuple-element.21.act_ref, f32[768,1536]{1,0:T(8,128)S(1)} %near_part.4.base_ref, bf16[256,1536]{1,0:T(8,128)(2,1)S(1)} %collective-permute-done.9.refs_0_.refs_5_, bf16[256,1536]{1,0:T(8,128)(2,1)S(1)} %collective-permute-done.10.refs_1_.refs_6_, ...), custom_call_target="tpu_custom_call" | custom-call | flops 28311552 | bytes 131072 | tf_op jit(solution)/shard_map/near_part/pallas_call | solution.py:204
  39.4 4.4 %out_grads.1 = (bf16[768,1536]{1,0:T(8,128)(2,1)S(1)}, bf16[256,1536]{1,0:T(8,128)(2,1)S(1)}, f32[256,1536]{1,0:T(8,128)S(1)}) custom-call(s32[2]{0:T(128)S(1)} %copy-done.8, f32[768,1536]{1,0:T(8,128)S(1)} %near_part.5.near_ref, bf16[768,2048]{1,0:T(8,128)(2,1)S(1)} %get-tuple-element.21.act_ref, f32[768,1536]{1,0:T(8,128)S(1)} %get-tuple-element.29.target_ref, ...), custom_call_target="tpu_custom_call" | custom-call | flops 18874368 | bytes 245760 | tf_op jit(solution)/shard_map/out_grads/pallas_call | solution.py:263
  44.1 2.0 %outer.2.refs_0_ = bf16[768,1536]{1,0:T(8,128)(2,1)S(1)} custom-call(bf16[2048,768]{1,0:T(8,128)(2,1)S(1)} %get-tuple-element.22.after_ref.refs_1_.refs_0_, bf16[768,1536]{1,0:T(8,128)(2,1)S(1)} %get-tuple-element.30.refs_1_.grad_ref, bf16[256,1536]{1,0:T(8,128)(2,1)S(1)} %get-tuple-element.31.refs_2_), custom_call_target="tpu_custom_call" | custom-call | flops 28311552 | bytes 65536 | tf_op jit(solution)/shard_map/outer/pallas_call | solution.py:306
  46.8 2.5 %collective-permute-start.16 = (bf16[256,1536]{1,0:T(8,128)(2,1)S(1)}, bf16[256,1536]{1,0:T(8,128)(2,1)S(1)}, u32[]{:S(2)}, u32[]{:S(2)}) collective-permute-start(bf16[256,1536]{1,0:T(8,128)(2,1)S(1)} %add_convert_fusion.refs_3_), channel_id=1, source_target_pairs={{0,128},{8,40},{16,144},{24,56},{32,160},{40,8},{48,176},{56,24},{... | collective-permute-start | bytes 2359304 | tf_op jit(solution)/shard_map/ppermute | solution.py:31
  49.3 1.5 %collective-permute-done.13.refs_2_ = bf16[768,1536]{1,0:T(8,128)(2,1)S(1)} collective-permute-done((bf16[768,1536]{1,0:T(8,128)(2,1)S(1)}, bf16[768,1536]{1,0:T(8,128)(2,1)S(1)}, u32[]{:S(2)}, u32[]{:S(2)}) %collective-permute-start.13) | collective-permute-done | bytes 2359328 | tf_op jit(solution)/shard_map/ppermute | solution.py:20
  50.7 2.0 %outer.3 = (bf16[256,1536]{1,0:T(8,128)(2,1)S(1)}, bf16[256,1536]{1,0:T(8,128)(2,1)S(1)}, f32[256,1536]{1,0:T(8,128)S(1)}) custom-call(bf16[2048,768]{1,0:T(8,128)(2,1)S(1)} %get-tuple-element.22.after_ref.refs_1_.refs_0_, bf16[768,1536]{1,0:T(8,128)(2,1)S(1)} %get-tuple-element.30.refs_1_.grad_ref, bf16[768,1536]{1,0:T(8,128)(2,1)S(1)} %collective-permute-done.13.refs_2_, ...), custom_call_target="tpu_custom_call" | custom-call | flops 28311552 | bytes 65536 | tf_op jit(solution)/shard_map/outer/pallas_call | solution.py:306
  52.7 1.5 %collective-permute-start.14 = (bf16[256,1536]{1,0:T(8,128)(2,1)S(1)}, bf16[256,1536]{1,0:T(8,128)(2,1)S(1)}, u32[]{:S(2)}, u32[]{:S(2)}) collective-permute-start(bf16[256,1536]{1,0:T(8,128)(2,1)S(1)} %get-tuple-element.33.refs_8_), channel_id=1, source_target_pairs={{0,64},{8,24},{16,80},{24,40},{32,96},{40,56},{48,112},{56,8},{64,... | collective-permute-start | bytes 2359304 | tf_op jit(solution)/shard_map/ppermute | solution.py:31
  54.2 1.8 %collective-permute-start.15 = (bf16[256,1536]{1,0:T(8,128)(2,1)S(1)}, bf16[256,1536]{1,0:T(8,128)(2,1)S(1)}, u32[]{:S(2)}, u32[]{:S(2)}) collective-permute-start(bf16[256,1536]{1,0:T(8,128)(2,1)S(1)} %get-tuple-element.35.refs_0_), channel_id=1, source_target_pairs={{0,192},{8,56},{16,208},{24,8},{32,224},{40,24},{48,240},{56,40},{... | collective-permute-start | bytes 2359304 | tf_op jit(solution)/shard_map/ppermute | solution.py:31
  56.0 1.0 whole_weight.1.w_ref
  57.1 6.1 %pre_grads.2 = (bf16[768,2048]{1,0:T(8,128)(2,1)}, f32[8,128]{1,0:T(8,128)S(1)}) custom-call(bf16[768,1536]{1,0:T(8,128)(2,1)S(1)} %get-tuple-element.30.refs_1_.grad_ref, bf16[2048,1536]{1,0:T(8,128)(2,1)S(1)} %whole_weight.1.w_ref, bf16[768,2048]{1,0:T(8,128)(2,1)S(1)} %bitcast.8, bf16[256,1536]{1,0:T(8,128)(2,1)S(1)} %get-tuple-element.35.refs_0_), custom_call_target="tpu_custom_call" | custom-call | flops 56623104 | bytes 196608 | tf_op jit(solution)/shard_map/pre_grads/pallas_call | solution.py:373
  63.2 5.6 %collective-permute-done.14 = bf16[256,1536]{1,0:T(8,128)(2,1)S(1)} collective-permute-done((bf16[256,1536]{1,0:T(8,128)(2,1)S(1)}, bf16[256,1536]{1,0:T(8,128)(2,1)S(1)}, u32[]{:S(2)}, u32[]{:S(2)}) %collective-permute-start.14) | collective-permute-done | bytes 786464 | tf_op jit(solution)/shard_map/ppermute | solution.py:31
  69.3 1.9 %collective-permute-start.17 = (bf16[64,1536]{1,0:T(8,128)(2,1)S(1)}, bf16[64,1536]{1,0:T(8,128)(2,1)S(1)}, u32[]{:S(2)}, u32[]{:S(2)}) collective-permute-start(bf16[64,1536]{1,0:T(8,128)(2,1)S(1)} %get-tuple-element.42), channel_id=1, source_target_pairs={{0,16},{8,72},{16,32},{24,88},{32,48},{40,104},{48,0},{56,120},{64... | collective-permute-start | bytes 589832 | tf_op jit(solution)/shard_map/ppermute | solution.py:31
  71.2 1.2 %collective-permute-start.19 = (bf16[64,1536]{1,0:T(8,128)(2,1)S(1)}, bf16[64,1536]{1,0:T(8,128)(2,1)S(1)}, u32[]{:S(2)}, u32[]{:S(2)}) collective-permute-start(bf16[64,1536]{1,0:T(8,128)(2,1)S(1)} %get-tuple-element.43), channel_id=1, source_target_pairs={{0,32},{8,136},{16,48},{24,152},{32,0},{40,168},{48,16},{56,184},{... | collective-permute-start | bytes 589832 | tf_op jit(solution)/shard_map/ppermute | solution.py:31
  72.9 2.5 %pre_grads.3 = (bf16[768,2048]{1,0:T(8,128)(2,1)}, f32[8,128]{1,0:T(8,128)S(1)}) custom-call(bf16[768,1536]{1,0:T(8,128)(2,1)S(1)} %get-tuple-element.30.refs_1_.grad_ref, bf16[2048,1536]{1,0:T(8,128)(2,1)S(1)} %whole_weight.1.w_ref, bf16[768,2048]{1,0:T(8,128)(2,1)S(1)} %bitcast.9, ...), custom_call_target="tpu_custom_call", output_to_operand_aliasing={{0}: (4, {})} | custom-call | flops 18874368 | bytes 65536 | tf_op jit(solution)/shard_map/pre_grads/pallas_call | solution.py:373
  75.4 1.1 collective-permute-done.17
  76.5 1.9 %collective-permute-done.19 = bf16[64,1536]{1,0:T(8,128)(2,1)S(1)} collective-permute-done((bf16[64,1536]{1,0:T(8,128)(2,1)S(1)}, bf16[64,1536]{1,0:T(8,128)(2,1)S(1)}, u32[]{:S(2)}, u32[]{:S(2)}) %collective-permute-start.19) | collective-permute-done | bytes 196640 | tf_op jit(solution)/shard_map/ppermute | solution.py:31
  78.5 2.0 %collective-permute-done.18 = bf16[64,1536]{1,0:T(8,128)(2,1)S(1)} collective-permute-done((bf16[64,1536]{1,0:T(8,128)(2,1)S(1)}, bf16[64,1536]{1,0:T(8,128)(2,1)S(1)}, u32[]{:S(2)}, u32[]{:S(2)}) %collective-permute-start.18) | collective-permute-done | bytes 196640 | tf_op jit(solution)/shard_map/ppermute | solution.py:31
  80.6 18.0 %all_to_all.15 = bf16[8,8,1536]{2,1,0:T(8,128)(2,1)S(1)} all-to-all(bf16[8,8,1536]{2,1,0:T(8,128)(2,1)S(1)} %fusion), channel_id=1, replica_groups=mesh['y'=4,'x'=4,'c'=2,'z'=8] {'z'}, dimensions={0} | all-to-all | bytes 393216 | tf_op jit(solution)/shard_map/all_to_all | solution.py:434
  98.7 12.2 %all_to_all.16 = bf16[8,8,1536]{2,1,0:T(8,128)(2,1)S(1)} all-to-all(bf16[8,8,1536]{2,1,0:T(8,128)(2,1)S(1)} %broadcast_in_dim.2), channel_id=1, replica_groups=mesh['y'=4,'x'=4,'c'=2,'z'=8] {'z'}, dimensions={0} | all-to-all | bytes 393216 | tf_op jit(solution)/shard_map/all_to_all | solution.py:437
  (54 shorter events, 6.7 us)
Async XLA Ops:
  0.6 9.6 %collective-permute-start.1 = (bf16[64,1536]{1,0:T(8,128)(2,1)}, bf16[64,1536]{1,0:T(8,128)(2,1)S(1)}, u32[]{:S(2)}, u32[]{:S(2)}) collective-permute-start(bf16[64,1536]{1,0:T(8,128)(2,1)} %own_ref.1), channel_id=1, source_target_pairs={{0,48},{8,200},{16,0},{24,216},{32,16},{40,232},{48,32},{56,248},{... | collective-permute-start | bytes 589832 | tf_op jit(solution)/shard_map/ppermute | solution.py:31
  1.5 8.7 %collective-permute-start = (bf16[64,1536]{1,0:T(8,128)(2,1)}, bf16[64,1536]{1,0:T(8,128)(2,1)S(1)}, u32[]{:S(2)}, u32[]{:S(2)}) collective-permute-start(bf16[64,1536]{1,0:T(8,128)(2,1)} %own_ref.1), channel_id=1, source_target_pairs={{0,16},{8,72},{16,32},{24,88},{32,48},{40,104},{48,0},{56,120},{64... | collective-permute-start | bytes 589832 | tf_op jit(solution)/shard_map/ppermute | solution.py:31
  3.9 7.4 %collective-permute-start.2 = (bf16[64,1536]{1,0:T(8,128)(2,1)}, bf16[64,1536]{1,0:T(8,128)(2,1)S(1)}, u32[]{:S(2)}, u32[]{:S(2)}) collective-permute-start(bf16[64,1536]{1,0:T(8,128)(2,1)} %own_ref.1), channel_id=1, source_target_pairs={{0,32},{8,136},{16,48},{24,152},{32,0},{40,168},{48,16},{56,184},{... | collective-permute-start | bytes 589832 | tf_op jit(solution)/shard_map/ppermute | solution.py:31
  4.4 1.9 %copy-start = (bf16[2,6,64,2048]{3,2,1,0:T(8,128)(2,1)S(1)}, bf16[2,6,64,2048]{3,2,1,0:T(8,128)(2,1)}, u32[]{:S(2)}) copy-start(bf16[2,6,64,2048]{3,2,1,0:T(8,128)(2,1)} %param.13) | copy-start | bytes 9437188
  6.3 5.1 %copy-start.3 = (bf16[64,1536]{1,0:T(8,128)(2,1)S(1)}, bf16[64,1536]{1,0:T(8,128)(2,1)}, u32[]{:S(2)}) copy-start(bf16[64,1536]{1,0:T(8,128)(2,1)} %own_ref.1) | copy-start | bytes 589828
  11.3 5.5 %copy-start.2 = (bf16[2,3,32,1536]{3,2,1,0:T(8,128)(2,1)S(1)}, bf16[2,3,32,1536]{3,2,1,0:T(8,128)(2,1)}, u32[]{:S(2)}) copy-start(bf16[2,3,32,1536]{3,2,1,0:T(8,128)(2,1)} %mid_ref.1) | copy-start | bytes 1769476
  11.4 11.5 %copy-start.6 = (f32[1536]{0:T(1024)S(1)}, f32[1536]{0:T(1024)}, u32[]{:S(2)}) copy-start(f32[1536]{0:T(1024)} %base_ref.1) | copy-start | bytes 18436
  11.4 5.5 %collective-permute-start.3 = (bf16[256,1536]{1,0:T(8,128)(2,1)S(1)}, bf16[256,1536]{1,0:T(8,128)(2,1)S(1)}, u32[]{:S(2)}, u32[]{:S(2)}) collective-permute-start(bf16[256,1536]{1,0:T(8,128)(2,1)S(1)} %pack.1.refs_0_.refs_2_.after_ref.refs_3_), channel_id=1, source_target_pairs={{0,8},{8,0},{1,9},{9,1},{2,10},{10,2},{3,11},{11,3},{4,12},{12,4},... | collective-permute-start | bytes 2359304 | tf_op jit(solution)/shard_map/ppermute | solution.py:20
  11.6 21.9 %collective-permute-start.6 = (bf16[256,1536]{1,0:T(8,128)(2,1)S(1)}, bf16[256,1536]{1,0:T(8,128)(2,1)S(1)}, u32[]{:S(2)}, u32[]{:S(2)}) collective-permute-start(bf16[256,1536]{1,0:T(8,128)(2,1)S(1)} %pack.1.refs_0_.refs_2_.after_ref.refs_3_), channel_id=1, source_target_pairs={{0,64},{8,24},{16,80},{24,40},{32,96},{40,56},{48,112},{56,8},{64,... | collective-permute-start | bytes 2359304 | tf_op jit(solution)/shard_map/ppermute | solution.py:31
  13.2 20.3 %collective-permute-start.5 = (bf16[256,1536]{1,0:T(8,128)(2,1)S(1)}, bf16[256,1536]{1,0:T(8,128)(2,1)S(1)}, u32[]{:S(2)}, u32[]{:S(2)}) collective-permute-start(bf16[256,1536]{1,0:T(8,128)(2,1)S(1)} %pack.1.refs_0_.refs_2_.after_ref.refs_3_), channel_id=1, source_target_pairs={{0,192},{8,56},{16,208},{24,8},{32,224},{40,24},{48,240},{56,40},{... | collective-permute-start | bytes 2359304 | tf_op jit(solution)/shard_map/ppermute | solution.py:31
  14.9 19.6 %collective-permute-start.4 = (bf16[256,1536]{1,0:T(8,128)(2,1)S(1)}, bf16[256,1536]{1,0:T(8,128)(2,1)S(1)}, u32[]{:S(2)}, u32[]{:S(2)}) collective-permute-start(bf16[256,1536]{1,0:T(8,128)(2,1)S(1)} %pack.1.refs_0_.refs_2_.after_ref.refs_3_), channel_id=1, source_target_pairs={{0,128},{8,40},{16,144},{24,56},{32,160},{40,8},{48,176},{56,24},{... | collective-permute-start | bytes 2359304 | tf_op jit(solution)/shard_map/ppermute | solution.py:31
  16.9 13.7 %collective-permute-start.7 = (bf16[2,2,32,1536]{3,2,1,0:T(8,128)(2,1)S(1)}, bf16[2,2,32,1536]{3,2,1,0:T(8,128)(2,1)S(1)}, u32[]{:S(2)}, u32[]{:S(2)}) collective-permute-start(bf16[2,2,32,1536]{3,2,1,0:T(8,128)(2,1)S(1)} %get-tuple-element.23), channel_id=1, source_target_pairs={{0,1},{1,2},{2,3},{3,4},{4,5},{5,6},{6,7},{7,0},{8,9},{9,10},{10,1... | collective-permute-start | bytes 1179656 | tf_op jit(solution)/shard_map/ppermute | solution.py:20
  18.9 11.7 %collective-permute-start.8 = (bf16[2,2,32,1536]{3,2,1,0:T(8,128)(2,1)S(1)}, bf16[2,2,32,1536]{3,2,1,0:T(8,128)(2,1)S(1)}, u32[]{:S(2)}, u32[]{:S(2)}) collective-permute-start(bf16[2,2,32,1536]{3,2,1,0:T(8,128)(2,1)S(1)} %get-tuple-element.24), channel_id=1, source_target_pairs={{0,7},{1,0},{2,1},{3,2},{4,3},{5,4},{6,5},{7,6},{8,15},{9,8},{10,9... | collective-permute-start | bytes 1179656 | tf_op jit(solution)/shard_map/ppermute | solution.py:20
  22.9 7.6 %copy-start.4 = (f32[1536]{0:T(1024)S(1)}, f32[1536]{0:T(1024)}, u32[]{:S(2)}) copy-start(f32[1536]{0:T(1024)} %gain_ref.1) | copy-start | bytes 18436
  22.9 7.6 %copy-start.5 = (f32[1536]{0:T(1024)S(1)}, f32[1536]{0:T(1024)}, u32[]{:S(2)}) copy-start(f32[1536]{0:T(1024)} %bias_ref.1) | copy-start | bytes 18436
  22.9 7.6 %copy-start.7 = (s32[2,6]{1,0:T(2,128)S(1)}, s32[2,6]{1,0:T(2,128)}, u32[]{:S(2)}) copy-start(s32[2,6]{1,0:T(2,128)} %source_ref.1) | copy-start | bytes 148
  34.4 2.7 %collective-permute-start.9 = (bf16[256,1536]{1,0:T(8,128)(2,1)S(1)}, bf16[256,1536]{1,0:T(8,128)(2,1)S(1)}, u32[]{:S(2)}, u32[]{:S(2)}) collective-permute-start(bf16[256,1536]{1,0:T(8,128)(2,1)S(1)} %get-tuple-element.26.refs_0_.refs_1_), channel_id=1, source_target_pairs={{0,8},{8,0},{1,9},{9,1},{2,10},{10,2},{3,11},{11,3},{4,12},{12,4},... | collective-permute-start | bytes 2359304 | tf_op jit(solution)/shard_map/ppermute | solution.py:20
  34.5 3.4 %collective-permute-start.10 = (bf16[256,1536]{1,0:T(8,128)(2,1)S(1)}, bf16[256,1536]{1,0:T(8,128)(2,1)S(1)}, u32[]{:S(2)}, u32[]{:S(2)}) collective-permute-start(bf16[256,1536]{1,0:T(8,128)(2,1)S(1)} %get-tuple-element.27.refs_1_.refs_2_), channel_id=1, source_target_pairs={{0,8},{8,0},{1,9},{9,1},{2,10},{10,2},{3,11},{11,3},{4,12},{12,4},... | collective-permute-start | bytes 2359304 | tf_op jit(solution)/shard_map/ppermute | solution.py:20
  35.0 4.5 %collective-permute-start.11 = (bf16[256,1536]{1,0:T(8,128)(2,1)S(1)}, bf16[256,1536]{1,0:T(8,128)(2,1)S(1)}, u32[]{:S(2)}, u32[]{:S(2)}) collective-permute-start(bf16[256,1536]{1,0:T(8,128)(2,1)S(1)} %get-tuple-element.28.refs_2_.refs_0_), channel_id=1, source_target_pairs={{0,8},{8,0},{1,9},{9,1},{2,10},{10,2},{3,11},{11,3},{4,12},{12,4},... | collective-permute-start | bytes 2359304 | tf_op jit(solution)/shard_map/ppermute | solution.py:20
  37.2 2.2 %copy-start.8 = (s32[2]{0:T(128)S(1)}, s32[2]{0:T(128)}, u32[]{:S(2)}) copy-start(s32[2]{0:T(128)} %time_ref.1) | copy-start | bytes 28
  43.8 2.4 %collective-permute-start.12 = (bf16[256,1536]{1,0:T(8,128)(2,1)S(1)}, bf16[256,1536]{1,0:T(8,128)(2,1)S(1)}, u32[]{:S(2)}, u32[]{:S(2)}) collective-permute-start(bf16[256,1536]{1,0:T(8,128)(2,1)S(1)} %get-tuple-element.31.refs_2_), channel_id=1, source_target_pairs={{0,8},{8,0},{1,9},{9,1},{2,10},{10,2},{3,11},{11,3},{4,12},{12,4},... | collective-permute-start | bytes 2359304 | tf_op jit(solution)/shard_map/ppermute | solution.py:20
  46.2 4.5 %collective-permute-start.13 = (bf16[768,1536]{1,0:T(8,128)(2,1)S(1)}, bf16[768,1536]{1,0:T(8,128)(2,1)S(1)}, u32[]{:S(2)}, u32[]{:S(2)}) collective-permute-start(bf16[768,1536]{1,0:T(8,128)(2,1)S(1)} %gate.7), channel_id=1, source_target_pairs={{0,8},{8,0},{1,9},{9,1},{2,10},{10,2},{3,11},{11,3},{4,12},{12,4},... | collective-permute-start | bytes 7077896 | tf_op jit(solution)/shard_map/ppermute | solution.py:20
  46.8 16.4 %collective-permute-start.16 = (bf16[256,1536]{1,0:T(8,128)(2,1)S(1)}, bf16[256,1536]{1,0:T(8,128)(2,1)S(1)}, u32[]{:S(2)}, u32[]{:S(2)}) collective-permute-start(bf16[256,1536]{1,0:T(8,128)(2,1)S(1)} %add_convert_fusion.refs_3_), channel_id=1, source_target_pairs={{0,128},{8,40},{16,144},{24,56},{32,160},{40,8},{48,176},{56,24},{... | collective-permute-start | bytes 2359304 | tf_op jit(solution)/shard_map/ppermute | solution.py:31
  52.7 16.0 %collective-permute-start.14 = (bf16[256,1536]{1,0:T(8,128)(2,1)S(1)}, bf16[256,1536]{1,0:T(8,128)(2,1)S(1)}, u32[]{:S(2)}, u32[]{:S(2)}) collective-permute-start(bf16[256,1536]{1,0:T(8,128)(2,1)S(1)} %get-tuple-element.33.refs_8_), channel_id=1, source_target_pairs={{0,64},{8,24},{16,80},{24,40},{32,96},{40,56},{48,112},{56,8},{64,... | collective-permute-start | bytes 2359304 | tf_op jit(solution)/shard_map/ppermute | solution.py:31
  54.2 2.9 %copy-start.1 = (bf16[2,6,64,2048]{3,2,1,0:T(8,128)(2,1)S(1)}, bf16[2,6,64,2048]{3,2,1,0:T(8,128)(2,1)}, u32[]{:S(2)}) copy-start(bf16[2,6,64,2048]{3,2,1,0:T(8,128)(2,1)} %param.13) | copy-start | bytes 9437188
  54.2 14.5 %collective-permute-start.15 = (bf16[256,1536]{1,0:T(8,128)(2,1)S(1)}, bf16[256,1536]{1,0:T(8,128)(2,1)S(1)}, u32[]{:S(2)}, u32[]{:S(2)}) collective-permute-start(bf16[256,1536]{1,0:T(8,128)(2,1)S(1)} %get-tuple-element.35.refs_0_), channel_id=1, source_target_pairs={{0,192},{8,56},{16,208},{24,8},{32,224},{40,24},{48,240},{56,40},{... | collective-permute-start | bytes 2359304 | tf_op jit(solution)/shard_map/ppermute | solution.py:31
  69.3 7.2 %collective-permute-start.17 = (bf16[64,1536]{1,0:T(8,128)(2,1)S(1)}, bf16[64,1536]{1,0:T(8,128)(2,1)S(1)}, u32[]{:S(2)}, u32[]{:S(2)}) collective-permute-start(bf16[64,1536]{1,0:T(8,128)(2,1)S(1)} %get-tuple-element.42), channel_id=1, source_target_pairs={{0,16},{8,72},{16,32},{24,88},{32,48},{40,104},{48,0},{56,120},{64... | collective-permute-start | bytes 589832 | tf_op jit(solution)/shard_map/ppermute | solution.py:31
  71.2 7.3 %collective-permute-start.19 = (bf16[64,1536]{1,0:T(8,128)(2,1)S(1)}, bf16[64,1536]{1,0:T(8,128)(2,1)S(1)}, u32[]{:S(2)}, u32[]{:S(2)}) collective-permute-start(bf16[64,1536]{1,0:T(8,128)(2,1)S(1)} %get-tuple-element.43), channel_id=1, source_target_pairs={{0,32},{8,136},{16,48},{24,152},{32,0},{40,168},{48,16},{56,184},{... | collective-permute-start | bytes 589832 | tf_op jit(solution)/shard_map/ppermute | solution.py:31
  72.5 8.0 %collective-permute-start.18 = (bf16[64,1536]{1,0:T(8,128)(2,1)S(1)}, bf16[64,1536]{1,0:T(8,128)(2,1)S(1)}, u32[]{:S(2)}, u32[]{:S(2)}) collective-permute-start(bf16[64,1536]{1,0:T(8,128)(2,1)S(1)} %get-tuple-element.44), channel_id=1, source_target_pairs={{0,48},{8,200},{16,0},{24,216},{32,16},{40,232},{48,32},{56,248},{... | collective-permute-start | bytes 589832 | tf_op jit(solution)/shard_map/ppermute | solution.py:31
